TPU v7x, 32 devices: a whole 2x2x4 slice. The times are simulated.
32 devices in a mesh: row: 4 (over z), col: 8 (over y, x, core).
Axes of the slice: x: 2, y: 2, z: 4, core: 2. Of those that a mesh axis runs over, the one named last changes fastest.
Arguments:
- right_side: float32 [4096, 4, 128], P(('row', 'col')), may hold values from -60 to 60
- cluster_of: int32 [4096], P(('row', 'col')), may hold values from 0 to 4095, as said below
- near_rows: int32 [12288], P(('row', 'col')), may hold values from 0 to 127
- near_columns: int32 [12288], P(('row', 'col')), may hold values from 0 to 191, as said below
- near_blocks: bfloat16 [12288, 128, 128], P(('row', 'col')), may hold values from -1 to 1
- far_rows: int32 [32768], P(('row', 'col')), may hold values from 0 to 1023, as said below
- far_columns: int32 [32768], P(('row', 'col')), may hold values from 0 to 511
- far_rank: int32 [32768], P(('row', 'col')), may hold values from 4 to 16
- far_left: bfloat16 [32768, 16, 128], P(('row', 'col')), may hold values from -1.5 to 1.5
- far_right: bfloat16 [32768, 16, 128], P(('row', 'col')), may hold values from -0.5 to 0.5
Outputs:
- second_basis: float32 [4096, 4, 128], P(('row', 'col'))
- next_vector: float32 [4096, 4, 128], P(('row', 'col'))
- hessenberg: float32 [5, 4], replicated
Inputs may be any that keep to these rules, and one draw needn't show every extreme that they name: `cluster_of`: A permutation of the cluster positions; position g belongs to the device of index g // 128 along row+col. Each device's blocks go to at most 8 blocks a destination device, and exactly 8 to some. `near_columns`: position 32 is the device's own first block; entries never point before the first or after the last block of cluster order. `far_rows`: in each device's list, the k-th group of 128 entries has rows in blocks k * 128 to (k + 1) * 128 - 1 of the row cluster.
All inputs are finite; a program needn't handle non-finite values.
Results may differ from a plain program's by a relative error of at most 0.0018.
The roundings to bfloat16 on the way count: a program that leaves them out, or rounds other values in their place, can miss the bound.
Values may be sent and summed in bfloat16 or wider, within the bound.
A program may use at most 128 MiB of HBM per device.

v0:
```python
import functools

import jax
import jax.numpy as jnp
from jax import lax
from jax.experimental import pallas as pl
from jax.experimental.pallas import tpu as pltpu
from jax.sharding import PartitionSpec as P

epsilon = 1e-06
MESH = pl.DeviceIdType.MESH
HIGH = lax.Precision.HIGHEST
VMEM = pl.BlockSpec(memory_space=pltpu.VMEM)
LANES = 128
LIMIT = 56 * 2**20


def coordinates(index, column_count):
    return (lax.div(index, column_count), lax.rem(index, column_count))


def enter(me, rows, columns):
    count = rows * columns
    barrier = pltpu.get_barrier_semaphore()

    @pl.loop(1, count)
    def _(k):
        pl.semaphore_signal(
            barrier,
            inc=1,
            device_id=coordinates(lax.rem(me + k, count), columns),
            device_id_type=MESH,
        )

    pl.semaphore_wait(barrier, count - 1)


def exchange_kernel(rows, columns, send_ref, recv_ref, send_sem, recv_sem):
    count = rows * columns
    me = lax.axis_index("row") * columns + lax.axis_index("col")
    enter(me, rows, columns)

    def copy(k):
        peer = lax.rem(me + k, count)
        return pltpu.make_async_remote_copy(
            src_ref=send_ref.at[peer],
            dst_ref=recv_ref.at[me],
            send_sem=send_sem.at[k],
            recv_sem=recv_sem.at[k],
            device_id=coordinates(peer, columns),
            device_id_type=MESH,
        )

    def arrival(k):
        source = lax.rem(me + count - k, count)
        return pltpu.make_async_remote_copy(
            src_ref=send_ref.at[source],
            dst_ref=recv_ref.at[source],
            send_sem=send_sem.at[k],
            recv_sem=recv_sem.at[k],
            device_id=coordinates(source, columns),
            device_id_type=MESH,
        )

    @pl.loop(1, count)
    def _(k):
        copy(k).start()

    recv_ref[me] = send_ref[me]

    @pl.loop(1, count)
    def _(k):
        arrival(k).wait_recv()

    @pl.loop(1, count)
    def _(k):
        copy(k).wait_send()


def exchange(send, rows, columns, collective_id):
    count = rows * columns
    return pl.pallas_call(
        functools.partial(exchange_kernel, rows, columns),
        out_shape=jax.ShapeDtypeStruct(send.shape, send.dtype),
        in_specs=[VMEM],
        out_specs=VMEM,
        scratch_shapes=[
            pltpu.SemaphoreType.DMA((count,)),
            pltpu.SemaphoreType.DMA((count,)),
        ],
        compiler_params=pltpu.CompilerParams(
            collective_id=collective_id, has_side_effects=True, vmem_limit_bytes=LIMIT
        ),
    )(send)


def split_dot(picker, value):
    high = value.astype(jnp.bfloat16)
    rest = value - high.astype(jnp.float32)
    middle = rest.astype(jnp.bfloat16)
    low = (rest - middle.astype(jnp.float32)).astype(jnp.bfloat16)
    dot = functools.partial(jnp.dot, picker, preferred_element_type=jnp.float32)
    return dot(high) + (dot(middle) + dot(low))


def one_hot(condition):
    return jnp.where(condition, 1.0, 0.0).astype(jnp.bfloat16)


def remote(source, destination, sends, recvs, k, device):
    return pltpu.make_async_remote_copy(
        src_ref=source,
        dst_ref=destination,
        send_sem=sends.at[k],
        recv_sem=recvs.at[k],
        device_id=device,
        device_id_type=MESH,
    )


def near_group(sides, g, tables_ref, extended, near_ref, near_out, image):
    near_count = near_ref.shape[1]
    reach = extended.shape[0]
    blocks = image.shape[0]
    table = tables_ref[g]
    turned = table.T
    column = turned[:near_count, 0:1]
    pick = one_hot(
        column == lax.broadcasted_iota(jnp.int32, (near_count, reach), 1).astype(jnp.float32)
    )
    picked = jnp.dot(pick, extended[...], preferred_element_type=jnp.float32)
    batch = 8
    row_id = lax.rem(lax.broadcasted_iota(jnp.int32, (sides * batch, LANES), 0), batch)
    for j in range(near_count // batch):
        here = slice(j * batch, (j + 1) * batch)
        stacked = jnp.concatenate(
            [picked[here, s * LANES : (s + 1) * LANES] for s in range(sides)], axis=0
        ).astype(jnp.bfloat16)
        product = lax.dot_general(
            stacked,
            near_ref[g, here].reshape(batch * LANES, LANES),
            (((1,), (1,)), ((), ())),
            preferred_element_type=jnp.float32,
        )
        value = jnp.zeros((sides * batch, LANES), jnp.float32)
        for e in range(batch):
            value = jnp.where(row_id == e, product[:, e * LANES : (e + 1) * LANES], value)
        for s in range(sides):
            near_out[here, s * LANES : (s + 1) * LANES] = value[s * batch : (s + 1) * batch]
    place = one_hot(
        table[1:2, :near_count]
        == lax.broadcasted_iota(jnp.int32, (blocks, near_count), 0).astype(jnp.float32)
    )
    image[...] += split_dot(place, near_out[...])


def far_group(sides, g, tables_ref, everything, far_left, far_right, far_out):
    rows, blocks, width = everything.shape
    far_count, rank = far_left.shape[1:3]
    table = tables_ref[g]
    turned = table.T
    lanes = lax.broadcasted_iota(jnp.int32, (far_count, rows * blocks), 1).astype(jnp.float32)
    pick = one_hot(turned[:far_count, 2:3] == lanes)
    picked = jnp.dot(
        pick, everything[...].reshape(rows * blocks, width), preferred_element_type=jnp.float32
    )
    batch = 32
    shape = (sides * batch, batch * rank)
    entry = lax.rem(lax.broadcasted_iota(jnp.int32, shape, 0), batch)
    lane = lax.broadcasted_iota(jnp.int32, shape, 1)
    term = lax.rem(lane, rank).astype(jnp.float32)
    own_entry = lax.div(lane, rank) == entry
    for j in range(far_count // batch):
        here = slice(j * batch, (j + 1) * batch)
        stacked = jnp.concatenate(
            [picked[here, s * LANES : (s + 1) * LANES] for s in range(sides)], axis=0
        ).astype(jnp.bfloat16)
        product = lax.dot_general(
            stacked,
            far_right[g, here].reshape(batch * rank, LANES),
            (((1,), (1,)), ((), ())),
            preferred_element_type=jnp.float32,
        )
        ranks = jnp.concatenate([turned[here, 4:5]] * sides, axis=0)
        coefficients = jnp.where(own_entry & (term < ranks), product, 0.0).astype(jnp.bfloat16)
        value = jnp.dot(
            coefficients,
            far_left[g, here].reshape(batch * rank, LANES),
            preferred_element_type=jnp.float32,
        )
        for s in range(sides):
            far_out[here, s * LANES : (s + 1) * LANES] = value[s * batch : (s + 1) * batch]
    place = one_hot(
        table[3:4, :far_count]
        == lax.broadcasted_iota(jnp.int32, (blocks, far_count), 0).astype(jnp.float32)
    )
    return split_dot(place, far_out[...])


def arnoldi_kernel(
    rows,
    columns,
    first_ref,
    near_columns_ref,
    near_rows_ref,
    far_columns_ref,
    far_rows_ref,
    far_rank_ref,
    to_mesh_ref,
    to_own_ref,
    mesh_first_ref,
    near_hbm,
    far_left_hbm,
    far_right_hbm,
    basis_ref,
    next_ref,
    entries_ref,
    tables_ref,
    basis_back_ref,
    image_back_ref,
    flat,
    near_ref,
    far_left,
    far_right,
    own,
    basis,
    image,
    everything,
    extended,
    left,
    right,
    near_out,
    far_out,
    to_partner,
    from_partner,
    to_chips,
    from_chips,
    outgoing,
    outgoing_two,
    mine,
    parts,
    load_sem,
    halo_send,
    halo_recv,
    spread_send,
    spread_recv,
    pair_send,
    pair_recv,
    chip_send,
    chip_recv,
    sum_send,
    sum_recv,
    back_send,
    back_recv,
):
    row, column = lax.axis_index("row"), lax.axis_index("col")
    count = rows * columns
    me = row * columns + column
    blocks, width = first_ref.shape
    sides = width // LANES
    halo = left.shape[0]
    groups = near_ref.shape[0]
    pairs = columns // 2
    chip, core = lax.div(column, 2), lax.rem(column, 2)
    partner = 2 * chip + 1 - core
    panels = count * blocks * LANES
    lanes = [slice(s * LANES, (s + 1) * LANES) for s in range(sides)]
    capacity = outgoing.shape[1]

    def load(kind, g):
        source, target = (
            (near_hbm, near_ref),
            (far_left_hbm, far_left),
            (far_right_hbm, far_right),
        )[kind]
        return pltpu.make_async_copy(source.at[g], target.at[g], load_sem.at[kind, g])

    for kind in range(3):

        @pl.loop(0, groups)
        def _(g, kind=kind):
            load(kind, g).start()

    tables_ref[...] = jnp.zeros(tables_ref.shape, jnp.float32)
    for g in range(groups):
        for place, source in enumerate(
            (near_columns_ref, near_rows_ref, far_columns_ref, far_rows_ref, far_rank_ref)
        ):
            value = source[g : g + 1]
            if source is far_rows_ref:
                value = value - g * blocks
            tables_ref[g, place : place + 1, : source.shape[1]] = value.astype(jnp.float32)
    enter(me, rows, columns)

    def operate(a, between):
        after = coordinates(lax.rem(me + 1, count), columns)
        before = coordinates(lax.rem(me + count - 1, count), columns)
        halos = [
            remote(
                own.at[pl.ds(blocks - halo, halo)],
                left,
                halo_send.at[a],
                halo_recv.at[a],
                0,
                after,
            ),
            remote(own.at[pl.ds(0, halo)], right, halo_send.at[a], halo_recv.at[a], 1, before),
        ]
        for copy in halos:
            copy.start()
        everything[row] = own[...]

        def inside(index):
            return (index >= 0) & (index < rows)

        def hop(way, distance, slot):
            sign = 1 - 2 * way
            return remote(
                everything.at[slot],
                everything.at[slot],
                spread_send.at[a, way],
                spread_recv.at[a, way],
                distance,
                (lax.rem(row + sign + rows, rows), column),
            )

        def relay(distance):
            for way in range(2):
                sign = 1 - 2 * way
                source = row - sign * distance
                if distance > 0:

                    @pl.when(inside(source))
                    def _(way=way, source=source):
                        hop(way, distance - 1, source).wait_recv()

                if distance < rows - 1:

                    @pl.when(inside(source) & inside(row + sign))
                    def _(way=way, source=source):
                        hop(way, distance, source).start()

        relay(0)
        image[...] = 0.5 * own[...].astype(jnp.float32)
        extended[halo : halo + blocks] = own[...]
        for copy in halos:
            copy.wait()
        extended[0:halo] = left[...]
        extended[halo + blocks :] = right[...]

        @pl.loop(0, groups)
        def _(g):
            if a == 0:
                load(0, g).wait()
            near_group(sides, g, tables_ref, extended, near_ref, near_out, image)
            for distance in range(1, rows - 1):

                @pl.when(g == distance * groups // (rows - 1))
                def _(distance=distance):
                    relay(distance)

        relay(rows - 1)
        for way in range(2):
            sign = 1 - 2 * way
            for distance in range(rows - 1):
                source = row - sign * distance

                @pl.when(inside(source) & inside(row + sign))
                def _(way=way, source=source, distance=distance):
                    hop(way, distance, source).wait_send()

        between()
        if a == 0:
            for kind in (1, 2):

                @pl.loop(0, groups)
                def _(g, kind=kind):
                    load(kind, g).wait()

        far = functools.partial(
            far_group,
            sides,
            tables_ref=tables_ref,
            everything=everything,
            far_left=far_left,
            far_right=far_right,
            far_out=far_out,
        )

        def pair_copy(k, q):
            return remote(
                to_partner.at[q],
                from_partner.at[q],
                pair_send.at[a],
                pair_recv.at[a],
                k,
                (row, partner),
            )

        def chip_copy(k, q):
            return remote(
                to_chips.at[q],
                from_chips.at[chip],
                chip_send.at[a],
                chip_recv.at[a],
                k,
                (row, 2 * q + core),
            )

        @pl.loop(1, pairs + 1)
        def _(i):
            q = lax.rem(chip + i, pairs)
            k = i - 1
            to_partner[q] = far(2 * q + 1 - core)
            pair_copy(k, q).start()
            to_chips[q] = far(2 * q + core)
            pair_copy(k, q).wait_recv()
            to_chips[q] = to_chips[q] + from_partner[q]

            @pl.when(i < pairs)
            def _():
                chip_copy(k, q).start()

        image[...] += to_chips[chip]
        for i in range(1, pairs):
            source = lax.rem(chip + pairs - i, pairs)
            remote(
                to_chips.at[source],
                from_chips.at[source],
                chip_send.at[a],
                chip_recv.at[a],
                i - 1,
                (row, 2 * source + core),
            ).wait_recv()
            image[...] += from_chips[source]
        for i in range(1, pairs + 1):
            q = lax.rem(chip + i, pairs)
            pair_copy(i - 1, q).wait_send()
            if i < pairs:
                chip_copy(i - 1, q).wait_send()

    def all_sum(n, pairings):
        place = 0
        mine[n] = jnp.zeros(mine.shape[1:], jnp.float32)
        for one, two in pairings:
            for here in lanes:
                mine[n, place : place + 1] = jnp.sum(
                    one[:, here] * two[:, here], axis=0, keepdims=True
                )
                place += 1

        def copy(k, slot, peer):
            return remote(
                mine.at[n],
                parts.at[n, slot],
                sum_send.at[n],
                sum_recv.at[n],
                k,
                coordinates(peer, columns),
            )

        @pl.loop(1, count)
        def _(k):
            copy(k, me, lax.rem(me + k, count)).start()

        parts[n, me] = mine[n]

        @pl.loop(1, count)
        def _(k):
            source = lax.rem(me + count - k, count)
            copy(k, source, source).wait_recv()

        @pl.loop(1, count)
        def _(k):
            copy(k, me, lax.rem(me + k, count)).wait_send()

        return jnp.sum(jnp.sum(parts[n], axis=0), axis=1, keepdims=True) / panels

    def back(n, sent, landed):
        def copy(k, peer, slot):
            return remote(
                sent.at[peer],
                landed.at[slot],
                back_send.at[n],
                back_recv.at[n],
                k,
                coordinates(peer, columns),
            )

        def start(value):
            picked = split_dot(to_mesh_ref[...], value[...])
            for d in range(count):
                sent[d] = picked[d * capacity : (d + 1) * capacity]

            @pl.loop(1, count)
            def _(k):
                copy(k, lax.rem(me + k, count), me).start()

            landed[me] = sent[me]

        def wait():
            @pl.loop(1, count)
            def _(k):
                source = lax.rem(me + count - k, count)
                copy(k, source, source).wait_recv()

            @pl.loop(1, count)
            def _(k):
                copy(k, lax.rem(me + k, count), me).wait_send()

        return start, wait

    basis_start, basis_wait = back(0, outgoing, basis_back_ref)
    image_start, image_wait = back(1, outgoing_two, image_back_ref)

    own[...] = first_ref[...].astype(jnp.bfloat16)
    operate(0, lambda: None)
    project = all_sum(0, [(first_ref, image)])
    for s in range(sides):
        image[:, lanes[s]] = image[:, lanes[s]] - project[s : s + 1] * first_ref[:, lanes[s]]
    norm = jnp.sqrt(all_sum(1, [(image, image)]) + epsilon)
    for s in range(sides):
        value = image[:, lanes[s]] / norm[s : s + 1]
        basis[:, lanes[s]] = value
        own[:, lanes[s]] = value.astype(jnp.bfloat16)
    operate(1, lambda: basis_start(basis))
    image_start(image)
    projects = all_sum(2, [(first_ref, image), (basis, image)])

    def by_lane(column):
        shape = (column.shape[0], LANES)
        diagonal = lax.broadcasted_iota(jnp.int32, shape, 0) == lax.broadcasted_iota(
            jnp.int32, shape, 1
        )
        return jnp.sum(jnp.where(diagonal, column, 0.0), axis=0, keepdims=True)

    entries_ref[...] = jnp.zeros(entries_ref.shape, jnp.float32)
    found = (
        project[:sides],
        norm[:sides],
        projects[:sides],
        projects[sides : 2 * sides],
    )
    for place, value in enumerate(found):
        entries_ref[place : place + 1] = by_lane(value)

    def home(landed):
        for d in range(count):
            flat[d * capacity : (d + 1) * capacity] = landed[d]
        return split_dot(to_own_ref[...], flat[...])

    basis_wait()
    basis_ref[...] = home(basis_back_ref)
    image_wait()
    returned = home(image_back_ref)
    for s in range(sides):
        here = lanes[s]
        next_ref[:, here] = (
            returned[:, here]
            - projects[s : s + 1] * mesh_first_ref[:, here]
            - projects[sides + s : sides + s + 1] * basis_ref[:, here]
        )


def arnoldi(
    first, tables, to_mesh, to_own, mesh_first, near_blocks, far_left, far_right, rows, columns
):
    blocks, width = first.shape
    count = rows * columns
    groups = columns
    near_blocks = near_blocks.reshape(groups, -1, *near_blocks.shape[1:])
    far_left = far_left.reshape(groups, -1, *far_left.shape[1:])
    far_right = far_right.reshape(groups, -1, *far_right.shape[1:])
    halo = blocks // 4
    pairs = columns // 2
    dma = pltpu.SemaphoreType.DMA
    real, half = jnp.float32, jnp.bfloat16
    slots = (count, to_mesh.shape[0] // count, width)
    hbm = pl.BlockSpec(memory_space=pl.ANY)
    return pl.pallas_call(
        functools.partial(arnoldi_kernel, rows, columns),
        out_shape=[
            jax.ShapeDtypeStruct((blocks, width), real),
            jax.ShapeDtypeStruct((blocks, width), real),
            jax.ShapeDtypeStruct((8, LANES), real),
        ],
        in_specs=[VMEM] * 9 + [hbm] * 3,
        out_specs=[VMEM] * 3,
        scratch_shapes=[
            pltpu.VMEM((groups, 8, LANES), real),
            pltpu.VMEM(slots, real),
            pltpu.VMEM(slots, real),
            pltpu.VMEM((to_mesh.shape[0], width), real),
            pltpu.VMEM(near_blocks.shape, half),
            pltpu.VMEM(far_left.shape, half),
            pltpu.VMEM(far_right.shape, half),
            pltpu.VMEM((blocks, width), half),
            pltpu.VMEM((blocks, width), real),
            pltpu.VMEM((blocks, width), real),
            pltpu.VMEM((rows, blocks, width), half),
            pltpu.VMEM((blocks + 2 * halo, width), half),
            pltpu.VMEM((halo, width), half),
            pltpu.VMEM((halo, width), half),
            pltpu.VMEM((near_blocks.shape[1], width), real),
            pltpu.VMEM((far_left.shape[1], width), real),
            pltpu.VMEM((pairs, blocks, width), real),
            pltpu.VMEM((pairs, blocks, width), real),
            pltpu.VMEM((pairs, blocks, width), real),
            pltpu.VMEM((pairs, blocks, width), real),
            pltpu.VMEM(slots, real),
            pltpu.VMEM(slots, real),
            pltpu.VMEM((3, 8, LANES), real),
            pltpu.VMEM((3, count, 8, LANES), real),
            dma((3, groups)),
            dma((2, 2)),
            dma((2, 2)),
            dma((2, 2, rows - 1)),
            dma((2, 2, rows - 1)),
            dma((2, pairs)),
            dma((2, pairs)),
            dma((2, pairs)),
            dma((2, pairs)),
            dma((3, count)),
            dma((3, count)),
            dma((2, count)),
            dma((2, count)),
        ],
        compiler_params=pltpu.CompilerParams(
            collective_id=1, has_side_effects=True, vmem_limit_bytes=LIMIT
        ),
    )(first, *tables, to_mesh, to_own, mesh_first, near_blocks, far_left, far_right)


def body(
    right_side,
    cluster_of,
    near_rows,
    near_columns,
    near_blocks,
    far_rows,
    far_columns,
    far_rank,
    far_left,
    far_right,
):
    rows = lax.axis_size("row")
    columns = lax.axis_size("col")
    count = rows * columns
    blocks, sides, lanes = right_side.shape
    width = sides * lanes
    capacity = 2 * blocks // count
    panels = blocks * count * lanes
    far_count = far_rows.shape[0] // columns

    target = cluster_of // blocks
    place = cluster_of % blocks
    order = jnp.arange(blocks, dtype=jnp.int32)
    earlier = (target[None, :] == target[:, None]) & (order[None, :] < order[:, None])
    slot = target * capacity + jnp.sum(earlier.astype(jnp.int32), axis=1)
    slots = count * capacity
    to_slot = slot[None, :] == jnp.arange(slots, dtype=jnp.int32)[:, None]
    to_slot_f = to_slot.astype(jnp.float32)
    marks = jnp.sum(jnp.where(to_slot, place[None, :] + 1, 0), axis=1).astype(jnp.float32)

    lane = jnp.arange(lanes, dtype=jnp.int32)
    squares = jnp.sum(right_side * right_side, axis=(0, 2))
    half = lanes // 2
    step = half // sides
    square_lanes = jnp.repeat(squares, step)
    extra = jnp.concatenate(
        [
            jnp.broadcast_to(marks[:, None], (slots, half)),
            jnp.broadcast_to(square_lanes[None, :], (slots, half)),
        ],
        axis=1,
    )
    outgoing = jnp.dot(to_slot_f, right_side.reshape(blocks, width), precision=HIGH)
    arrived = exchange(
        jnp.concatenate([outgoing, extra], axis=1).reshape(count, capacity, width + lanes),
        rows,
        columns,
        0,
    )
    total = jnp.sum(arrived[:, 0, width + half :], axis=0).reshape(sides, step)[:, 0]
    side_norm = jnp.sqrt(total / panels + epsilon)
    arrived = arrived.reshape(slots, width + lanes)
    held = arrived[:, width].astype(jnp.int32) - 1
    from_slot = held[None, :] == order[:, None]
    to_cluster = from_slot.astype(jnp.float32)
    norm_lanes = jnp.repeat(side_norm, lanes)
    first = jnp.dot(to_cluster, arrived[:, :width], precision=HIGH) / norm_lanes[None, :]


    tables = [
        values.reshape(columns, -1)
        for values in (near_columns, near_rows, far_columns, far_rows, far_rank)
    ]
    to_mesh = (held[:, None] == order[None, :]).astype(jnp.bfloat16)
    to_own = (slot[:, None] == jnp.arange(slots, dtype=jnp.int32)[None, :]).astype(jnp.bfloat16)
    mesh_first = right_side.reshape(blocks, width) / norm_lanes[None, :]
    basis, following, entries = arnoldi(
        first,
        tables,
        to_mesh,
        to_own,
        mesh_first,
        near_blocks,
        far_left,
        far_right,
        rows,
        columns,
    )
    second_basis = basis.reshape(blocks, sides, lanes)
    next_vector = following.reshape(blocks, sides, lanes)
    hessenberg = jnp.concatenate([side_norm[None, :], entries[:4, :sides]], axis=0)
    return (second_basis, next_vector, hessenberg)


def solution(mesh):
    vector = P(("row", "col"), None, None)
    table = P(("row", "col"))
    placed = (vector, table, table, table, vector, table, table, table, vector, vector)
    return jax.shard_map(
        body,
        mesh=mesh,
        in_specs=placed,
        out_specs=(vector, vector, P()),
        check_vma=False,
    )
```

profile of v0, /device:TPU:0, one launch (start us, length us, event | category | flops | bytes accessed | tf_op | source)
XLA Modules:
  0.0 152.6 jit_solution(7624266901528233376)
XLA Ops:
  0.6 0.0 copy-start
  0.6 0.0 copy-start.1
  0.7 0.0 copy-start.2
  0.7 0.7 and_select_fusion.1
  1.4 0.2 convert_reduce_fusion
  1.6 1.3 fusion.1
  2.9 0.1 select_reduce_fusion
  3.0 0.1 broadcast_in_dim.24
  3.1 1.2 multiply_reduce_fusion
  4.3 0.1 broadcast_in_dim.25
  4.4 0.1 reshape.111
  4.5 0.1 pad.4.clone
  4.6 0.9 maximum_bitcast_fusion.send_ref
  5.5 20.6 %shard_map.121 = f32[32,8,640]{2,1,0:T(8,128)} custom-call(f32[32,8,640]{2,1,0:T(8,128)} %maximum_bitcast_fusion.send_ref), custom_call_target="tpu_custom_call" | custom-call | tf_op jit(solution)/shard_map/pallas_call | solution.py:82
  26.1 0.9 convert_add_fusion
  27.0 0.1 copy.20
  27.1 1.0 slice_reduce_fusion
  28.1 0.1 reshape.98
  28.2 0.1 sqrt_reduce_fusion
  28.3 0.1 broadcast_bitcast_fusion
  28.4 2.1 %convolution_divide_fusion.first_ref = f32[128,512]{1,0:T(8,128)} fusion(f32[256,640]{1,0:T(8,128)} %bitcast.24, f32[512]{0:T(512)S(1)} %broadcast_bitcast_fusion, s32[256]{0:T(256)S(1)} %bitcast.29), kind=kOutput, calls=%fused_computation | convolution fusion | flops 201424896 | bytes 789504 | tf_op jit(solution)/shard_map/dot_general | solution.py:691
  30.5 0.0 copy-done
  30.5 0.7 bitcast_divide_fusion.mesh_first_ref
  31.2 0.7 fusion.4.to_mesh_ref
  31.9 0.7 fusion.5.to_own_ref
  32.6 0.0 copy-done.1
  32.6 0.7 reshape.100.near_rows_ref
  33.3 0.0 copy-done.2
  33.3 0.7 reshape.99.near_columns_ref
  34.0 113.8 %shard_map.122 = (f32[128,512]{1,0:T(8,128)}, f32[128,512]{1,0:T(8,128)}, f32[8,128]{1,0:T(8,128)}) custom-call(f32[128,512]{1,0:T(8,128)} %convolution_divide_fusion.first_ref, s32[8,48]{1,0:T(8,128)} %reshape.99.near_columns_ref, s32[8,48]{1,0:T(8,128)} %reshape.100.near_rows_ref, s32[8,128]{1,0:T(8,128)} %bitcast.26, s32[8,128]{1,0:T(8,128)} %bitcast.27, ...), custom_call_target="tpu_custom_call" | custom-call | tf_op jit(solution)/shard_map/pallas_call | solution.py:580
  147.8 0.7 slice.19
  148.4 0.7 copy.17
  149.1 1.7 %reshape.107 = f32[128,4,128]{2,1,0:T(4,128)} reshape(f32[128,512]{1,0:T(8,128)} %get-tuple-element.6) | data formatting | bytes 524288 | tf_op jit(solution)/shard_map/reshape | solution.py:713
  150.9 1.7 %reshape.108 = f32[128,4,128]{2,1,0:T(4,128)} reshape(f32[128,512]{1,0:T(8,128)} %get-tuple-element.7) | data formatting | bytes 524288 | tf_op jit(solution)/shard_map/reshape | solution.py:714
  (3 shorter events, 0.0 us)
Async XLA Ops:
  0.6 29.8 %copy-start = (f32[128,4,128]{2,1,0:T(4,128)S(1)}, f32[128,4,128]{2,1,0:T(4,128)}, u32[]{:S(2)}) copy-start(f32[128,4,128]{2,1,0:T(4,128)} %param.10) | copy-start | bytes 786436
  0.6 32.0 %copy-start.1 = (s32[384]{0:T(512)S(1)}, s32[384]{0:T(512)}, u32[]{:S(2)}) copy-start(s32[384]{0:T(512)} %param.12) | copy-start | bytes 4612
  0.7 32.7 %copy-start.2 = (s32[384]{0:T(512)S(1)}, s32[384]{0:T(512)}, u32[]{:S(2)}) copy-start(s32[384]{0:T(512)} %param.13) | copy-start | bytes 4612
where the time goes:
time: 153 us
  Pallas kernels  134 us (88%)
  other arithmetic  7.36 us (5%)
  local copies, waits for them, and re-layouts  6.71 us (4%)
  matrix products  3.44 us (2%)
    pallas_call x1, Pallas kernels, arnoldi(): pl.pallas_call(functools.partial(arnoldi_kernel, rows, columns), out_shap...  114 us
    pallas_call x1, Pallas kernels, exchange(): pl.pallas_call(functools.partial(exchange_kernel, rows, columns), out_sha...  20.6 us

commit v1 on v0

v1 whole, which is shorter than its diff:
```python
import functools

import jax
import jax.numpy as jnp
from jax import lax
from jax.experimental import pallas as pl
from jax.experimental.pallas import tpu as pltpu
from jax.sharding import PartitionSpec as P

epsilon = 1e-06
MESH = pl.DeviceIdType.MESH
VMEM = pl.BlockSpec(memory_space=pltpu.VMEM)
LANES = 128
LIMIT = 56 * 2**20
TILE = 8
TOP = 32767.0


def coordinates(index, column_count):
    return (lax.div(index, column_count), lax.rem(index, column_count))


def enter(me, rows, columns):
    count = rows * columns
    barrier = pltpu.get_barrier_semaphore()

    @pl.loop(1, count)
    def _(k):
        pl.semaphore_signal(
            barrier,
            inc=1,
            device_id=coordinates(lax.rem(me + k, count), columns),
            device_id_type=MESH,
        )

    pl.semaphore_wait(barrier, count - 1)


def split_dot(picker, value, terms=3):
    total = None
    for _ in range(terms):
        part = value.astype(jnp.bfloat16)
        value = value - part.astype(jnp.float32)
        product = jnp.dot(picker, part, preferred_element_type=jnp.float32)
        total = product if total is None else total + product
    return total


def one_hot(condition):
    return jnp.where(condition, 1.0, 0.0).astype(jnp.bfloat16)


def remote(source, destination, sends, recvs, k, device):
    return pltpu.make_async_remote_copy(
        src_ref=source,
        dst_ref=destination,
        send_sem=sends.at[k],
        recv_sem=recvs.at[k],
        device_id=device,
        device_id_type=MESH,
    )


def near_group(sides, g, tables_ref, extended, near_ref, near_out, image):
    near_count = near_ref.shape[1]
    reach = extended.shape[0]
    blocks = image.shape[0]
    table = tables_ref[g]
    turned = table.T
    column = turned[:near_count, 0:1]
    pick = one_hot(
        column == lax.broadcasted_iota(jnp.int32, (near_count, reach), 1).astype(jnp.float32)
    )
    picked = jnp.dot(pick, extended[...], preferred_element_type=jnp.float32)
    batch = 8
    row_id = lax.rem(lax.broadcasted_iota(jnp.int32, (sides * batch, LANES), 0), batch)
    for j in range(near_count // batch):
        here = slice(j * batch, (j + 1) * batch)
        stacked = jnp.concatenate(
            [picked[here, s * LANES : (s + 1) * LANES] for s in range(sides)], axis=0
        ).astype(jnp.bfloat16)
        product = lax.dot_general(
            stacked,
            near_ref[g, here].reshape(batch * LANES, LANES),
            (((1,), (1,)), ((), ())),
            preferred_element_type=jnp.float32,
        )
        value = jnp.zeros((sides * batch, LANES), jnp.float32)
        for e in range(batch):
            value = jnp.where(row_id == e, product[:, e * LANES : (e + 1) * LANES], value)
        for s in range(sides):
            near_out[here, s * LANES : (s + 1) * LANES] = value[s * batch : (s + 1) * batch]
    place = one_hot(
        table[1:2, :near_count]
        == lax.broadcasted_iota(jnp.int32, (blocks, near_count), 0).astype(jnp.float32)
    )
    image[...] += split_dot(place, near_out[...])


def far_group(sides, g, tables_ref, everything, far_left, far_right, far_out):
    rows, blocks, width = everything.shape
    far_count, rank = far_left.shape[1:3]
    table = tables_ref[g]
    turned = table.T
    lanes = lax.broadcasted_iota(jnp.int32, (far_count, rows * blocks), 1).astype(jnp.float32)
    pick = one_hot(turned[:far_count, 0:1] == lanes)
    picked = jnp.dot(
        pick, everything[...].reshape(rows * blocks, width), preferred_element_type=jnp.float32
    )
    batch = 32
    shape = (sides * batch, batch * rank)
    entry = lax.rem(lax.broadcasted_iota(jnp.int32, shape, 0), batch)
    lane = lax.broadcasted_iota(jnp.int32, shape, 1)
    term = lax.rem(lane, rank).astype(jnp.float32)
    own_entry = lax.div(lane, rank) == entry
    for j in range(far_count // batch):
        here = slice(j * batch, (j + 1) * batch)
        stacked = jnp.concatenate(
            [picked[here, s * LANES : (s + 1) * LANES] for s in range(sides)], axis=0
        ).astype(jnp.bfloat16)
        product = lax.dot_general(
            stacked,
            far_right[g, here].reshape(batch * rank, LANES),
            (((1,), (1,)), ((), ())),
            preferred_element_type=jnp.float32,
        )
        ranks = jnp.concatenate([turned[here, 2:3]] * sides, axis=0)
        coefficients = jnp.where(own_entry & (term < ranks), product, 0.0).astype(jnp.bfloat16)
        value = jnp.dot(
            coefficients,
            far_left[g, here].reshape(batch * rank, LANES),
            preferred_element_type=jnp.float32,
        )
        for s in range(sides):
            far_out[here, s * LANES : (s + 1) * LANES] = value[s * batch : (s + 1) * batch]
    place = one_hot(
        table[1:2, :far_count]
        == lax.broadcasted_iota(jnp.int32, (blocks, far_count), 0).astype(jnp.float32)
    )
    return split_dot(place, far_out[...])


def iota(shape, dimension):
    return lax.broadcasted_iota(jnp.int32, shape, dimension)


def encode(value, scale):
    code = jnp.floor(jnp.clip(value * (TOP / scale), -TOP, TOP) + 0.5)
    return code.astype(jnp.int32).astype(jnp.int16)


def decode(code):
    return code.astype(jnp.int32).astype(jnp.float32)


def largest(value):
    top = jnp.max(jnp.abs(value), axis=0, keepdims=True)
    return jnp.maximum(jnp.max(top, axis=1, keepdims=True), 1e-30)


def total_of(value):
    return jnp.sum(jnp.sum(value, axis=0, keepdims=True), axis=1, keepdims=True)


def arnoldi_kernel(
    rows,
    columns,
    side_ref,
    cluster_ref,
    near_columns_ref,
    near_rows_ref,
    far_columns_ref,
    far_rows_ref,
    far_rank_ref,
    near_hbm,
    far_left_hbm,
    far_right_hbm,
    basis_ref,
    next_ref,
    entries_ref,
    near_tables,
    far_tables,
    sent,
    landed,
    sent_basis,
    landed_basis,
    sent_image,
    landed_image,
    first_ref,
    near_ref,
    far_left,
    far_right,
    own,
    basis,
    image,
    everything,
    extended,
    left,
    right,
    near_out,
    far_out,
    to_partner,
    from_partner,
    to_chips,
    from_chips,
    code_to,
    code_from,
    scale_to,
    scale_from,
    mine,
    parts,
    load_sem,
    halo_send,
    halo_recv,
    spread_send,
    spread_recv,
    pair_send,
    pair_recv,
    chip_send,
    chip_recv,
    scale_send,
    scale_recv,
    all_send,
    all_recv,
):
    row, column = lax.axis_index("row"), lax.axis_index("col")
    count = rows * columns
    me = row * columns + column
    blocks, width = first_ref.shape
    sides = width // LANES
    halo = left.shape[0]
    groups = far_left.shape[0]
    near_groups = near_ref.shape[0]
    pairs = columns // 2
    chip, core = lax.div(column, 2), lax.rem(column, 2)
    partner = 2 * chip + 1 - core
    panels = count * blocks * LANES
    lanes = [slice(s * LANES, (s + 1) * LANES) for s in range(sides)]
    capacity = (sent.shape[1] - TILE) // sides
    slots = count * capacity
    lane_row = iota((1, LANES), 1)

    def load(kind, g):
        source, target = (
            (near_hbm, near_ref),
            (far_left_hbm, far_left),
            (far_right_hbm, far_right),
        )[kind]
        return pltpu.make_async_copy(source.at[g], target.at[g], load_sem.at[kind, g])

    for kind, many in enumerate((near_groups, groups, groups)):

        @pl.loop(0, many)
        def _(g, kind=kind):
            load(kind, g).start()

    def to_all(n, source, destination, part):
        def copy(peer, there, here):
            return pltpu.make_async_remote_copy(
                src_ref=source.at[there, part],
                dst_ref=destination.at[here, part],
                send_sem=all_send.at[n],
                recv_sem=all_recv.at[n],
                device_id=coordinates(peer, columns),
                device_id_type=MESH,
            )

        def start():
            @pl.loop(1, count)
            def _(k):
                peer = lax.rem(me + k, count)
                copy(peer, peer, me).start()

            destination[me] = source[me]

        every = copy(lax.rem(me + 1, count), pl.ds(0, count - 1), pl.ds(0, count - 1))
        return start, every.wait_recv, every.wait_send

    def share(n, values):
        row_of = jnp.zeros((1, LANES), jnp.float32)
        for place, value in enumerate(values):
            row_of = row_of + jnp.where(lane_row == place, value, 0.0)
        mine[n] = jnp.broadcast_to(row_of, (TILE, LANES))

        def copy(peer, here):
            return pltpu.make_async_remote_copy(
                src_ref=mine.at[n] if here is not None else parts.at[n, pl.ds(0, count - 1)],
                dst_ref=parts.at[n, here if here is not None else pl.ds(0, count - 1)],
                send_sem=all_send.at[3 + n],
                recv_sem=all_recv.at[3 + n],
                device_id=coordinates(peer, columns),
                device_id_type=MESH,
            )

        @pl.loop(1, count)
        def _(k):
            copy(lax.rem(me + k, count), me).start()

        parts[n, me] = mine[n]
        every = copy(lax.rem(me + 1, count), None)

        def wait():
            every.wait_recv()
            every.wait_send()
            return parts[n, :, 0, :]

        return wait

    def single(total, place):
        return jnp.sum(jnp.where(lane_row == place, total, 0.0), axis=1, keepdims=True)

    cluster = cluster_ref[...]
    target = lax.div(cluster, blocks)
    turned = jnp.broadcast_to(cluster.astype(jnp.float32), (blocks, blocks)).T.astype(jnp.int32)
    turned_target = lax.div(turned, blocks)
    place = turned - turned_target * blocks
    square = (blocks, blocks)
    same = turned_target == target
    ranks = jnp.where(same & (iota(square, 1) < iota(square, 0)), 1, 0)
    rank_column = jnp.sum(ranks, axis=1, keepdims=True)
    ranks = jnp.where(same & (iota(square, 0) < iota(square, 1)), 1, 0)
    rank_row = jnp.sum(ranks, axis=0, keepdims=True)
    slot_shape = (slots, blocks)
    to_slot = one_hot(iota(slot_shape, 0) == target * capacity + rank_row)
    to_device = one_hot(lax.div(iota(slot_shape, 0), capacity) == target)
    marks = jnp.where(iota(square, 1) == rank_column, place + 1, 0)
    extra = jnp.dot(
        to_device,
        marks.astype(jnp.float32).astype(jnp.bfloat16),
        preferred_element_type=jnp.float32,
    )
    stride = [pl.ds(s, blocks, stride=sides) for s in range(sides)]
    for s in range(sides):
        value = side_ref[stride[s], :]
        extra = extra + jnp.where(lane_row == capacity + s, total_of(value * value), 0.0)
        picked = split_dot(to_slot, value)
        sent[:, s * capacity : (s + 1) * capacity, :] = picked.reshape(count, capacity, LANES)
    top = sides * capacity
    if capacity == TILE:
        sent[:, top:, :] = extra.reshape(count, TILE, LANES)
    else:
        sent[:, top:, :] = extra.reshape(count, capacity, LANES)[:, :TILE]
    enter(me, rows, columns)
    out_start, out_recv, out_send = to_all(0, sent, landed, pl.ds(0, top + TILE))
    out_start()

    near_tables[...] = jnp.zeros(near_tables.shape, jnp.float32)
    for g in range(near_groups):
        for spot, source in enumerate((near_columns_ref, near_rows_ref)):
            near_tables[g, spot : spot + 1] = source[g : g + 1].astype(jnp.float32)
    far_tables[...] = jnp.zeros(far_tables.shape, jnp.float32)
    for g in range(groups):
        for spot, source in enumerate((far_columns_ref, far_rows_ref, far_rank_ref)):
            value = source[g : g + 1]
            if source is far_rows_ref:
                value = value - g * blocks
            far_tables[g, spot : spot + 1, : source.shape[1]] = value.astype(jnp.float32)

    out_recv()
    table = landed[:, top, :]
    total = jnp.sum(table, axis=0, keepdims=True)
    norms = [
        jnp.sqrt(single(total, capacity + s) / panels + epsilon) for s in range(sides)
    ]
    spread_marks = jnp.dot(
        one_hot(lax.div(iota((slots, count), 0), capacity) == iota((slots, count), 1)),
        jnp.where(iota((count, LANES), 1) < capacity, table, 0.0).astype(jnp.bfloat16),
        preferred_element_type=jnp.float32,
    )
    wide = (slots, LANES)
    held = jnp.sum(
        jnp.where(lax.rem(iota(wide, 0), capacity) == iota(wide, 1), spread_marks, 0.0),
        axis=1,
        keepdims=True,
    ).astype(jnp.int32) - 1
    to_mesh_wide = jnp.where(held == iota((slots, blocks), 1), 1.0, 0.0)
    to_mesh = to_mesh_wide.astype(jnp.bfloat16)
    to_cluster = to_mesh_wide.T.astype(jnp.bfloat16)
    for s in range(sides):
        arrived = landed[:, s * capacity : (s + 1) * capacity, :].reshape(slots, LANES)
        value = split_dot(to_cluster, arrived) / norms[s]
        first_ref[:, lanes[s]] = value
        own[:, lanes[s]] = value.astype(jnp.bfloat16)
    out_send()

    def operate(a, between):
        after = coordinates(lax.rem(me + 1, count), columns)
        before = coordinates(lax.rem(me + count - 1, count), columns)
        halos = [
            remote(
                own.at[pl.ds(blocks - halo, halo)],
                left,
                halo_send.at[a],
                halo_recv.at[a],
                0,
                after,
            ),
            remote(own.at[pl.ds(0, halo)], right, halo_send.at[a], halo_recv.at[a], 1, before),
        ]
        for copy in halos:
            copy.start()
        everything[row] = own[...]

        def inside(index):
            return (index >= 0) & (index < rows)

        def hop(way, distance, slot):
            sign = 1 - 2 * way
            return remote(
                everything.at[slot],
                everything.at[slot],
                spread_send.at[a, way],
                spread_recv.at[a, way],
                distance,
                (lax.rem(row + sign + rows, rows), column),
            )

        def relay(distance):
            for way in range(2):
                sign = 1 - 2 * way
                source = row - sign * distance
                if distance > 0:

                    @pl.when(inside(source))
                    def _(way=way, source=source):
                        hop(way, distance - 1, source).wait_recv()

                if distance < rows - 1:

                    @pl.when(inside(source) & inside(row + sign))
                    def _(way=way, source=source):
                        hop(way, distance, source).start()

        relay(0)
        image[...] = 0.5 * own[...].astype(jnp.float32)
        extended[halo : halo + blocks] = own[...]
        for copy in halos:
            copy.wait()
        extended[0:halo] = left[...]
        extended[halo + blocks :] = right[...]

        @pl.loop(0, near_groups)
        def _(g):
            if a == 0:
                load(0, g).wait()
            near_group(sides, g, near_tables, extended, near_ref, near_out, image)
            for distance in range(1, rows - 1):

                @pl.when(g == distance * near_groups // (rows - 1))
                def _(distance=distance):
                    relay(distance)

        relay(rows - 1)
        for way in range(2):
            sign = 1 - 2 * way
            for distance in range(rows - 1):
                source = row - sign * distance

                @pl.when(inside(source) & inside(row + sign))
                def _(way=way, source=source, distance=distance):
                    hop(way, distance, source).wait_send()

        between()
        if a == 0:
            for kind in (1, 2):

                @pl.loop(0, groups)
                def _(g, kind=kind):
                    load(kind, g).wait()

        far = functools.partial(
            far_group,
            sides,
            tables_ref=far_tables,
            everything=everything,
            far_left=far_left,
            far_right=far_right,
            far_out=far_out,
        )

        def pair_copy(k, q):
            return remote(
                to_partner.at[q],
                from_partner.at[q],
                pair_send.at[a],
                pair_recv.at[a],
                k,
                (row, partner),
            )

        def chip_copies(k, q, here):
            device = (row, 2 * q + core)
            if a == 0:
                return [
                    remote(
                        to_chips.at[q],
                        from_chips.at[here],
                        chip_send.at[a],
                        chip_recv.at[a],
                        k,
                        device,
                    )
                ]
            return [
                remote(
                    code_to.at[q],
                    code_from.at[here],
                    chip_send.at[a],
                    chip_recv.at[a],
                    k,
                    device,
                ),
                remote(scale_to.at[q], scale_from.at[here], scale_send, scale_recv, k, device),
            ]

        @pl.loop(1, pairs + 1)
        def _(i):
            q = lax.rem(chip + i, pairs)
            k = i - 1
            to_partner[q] = far(2 * q + 1 - core)
            pair_copy(k, q).start()
            to_chips[q] = far(2 * q + core)
            pair_copy(k, q).wait_recv()
            to_chips[q] = to_chips[q] + from_partner[q]

            @pl.when(i < pairs)
            def _():
                if a == 1:
                    for s in range(sides):
                        value = to_chips[q, :, lanes[s]]
                        scale = jnp.max(jnp.abs(value), axis=0, keepdims=True)
                        scale = jnp.maximum(scale, 1e-30)
                        scale_to[q, s * TILE : (s + 1) * TILE] = jnp.broadcast_to(
                            scale, (TILE, LANES)
                        )
                        code_to[q, :, lanes[s]] = encode(value, scale)
                for copy in chip_copies(k, q, chip):
                    copy.start()

        image[...] += to_chips[chip]
        for i in range(1, pairs):
            source = lax.rem(chip + pairs - i, pairs)
            for copy in chip_copies(i - 1, source, source):
                copy.wait_recv()
            if a == 0:
                image[...] += from_chips[source]
            else:
                for s in range(sides):
                    scale = scale_from[source, s * TILE : s * TILE + 1] * (1.0 / TOP)
                    image[:, lanes[s]] += decode(code_from[source, :, lanes[s]]) * scale
        for i in range(1, pairs + 1):
            q = lax.rem(chip + i, pairs)
            pair_copy(i - 1, q).wait_send()
            if i < pairs:
                for copy in chip_copies(i - 1, q, chip):
                    copy.wait_send()

    def slot_codes(value, scales, buffer):
        for s in range(0, sides, 2):
            codes = []
            for side in (s, s + 1):
                code = jnp.floor(
                    jnp.clip(value[:, lanes[side]] * (TOP / scales[side]), -TOP, TOP) + 0.5
                )
                codes.append(split_dot(to_mesh, code, 2).reshape(count, capacity, LANES))
            both = jnp.concatenate(codes, axis=1)
            buffer[:, s * capacity : (s + 2) * capacity, :] = both.astype(jnp.int32).astype(
                jnp.int16
            )

    to_own = one_hot(
        turned_target[:, 0:1] * capacity + rank_column == iota((blocks, slots), 1)
    )
    to_source = one_hot(turned_target[:, 0:1] == iota((blocks, count), 1))

    def home(buffer, scales):
        values = []
        own_scales = split_dot(to_source, scales)
        for s in range(0, sides, 2):
            both = decode(buffer[:, s * capacity : (s + 2) * capacity, :])
            for side in (s, s + 1):
                code = both[:, (side - s) * capacity : (side - s + 1) * capacity]
                value = split_dot(to_own, code.reshape(slots, LANES), 2)
                values.append(value * (own_scales[:, side : side + 1] * (1.0 / TOP)))
        return values

    operate(0, lambda: None)
    found = [[] for _ in range(7)]
    for s in range(sides):
        one, two = first_ref[:, lanes[s]], image[:, lanes[s]]
        along, size = total_of(one * two), total_of(one * one)
        guess = jnp.where(size > 1e-30, along / jnp.maximum(size, 1e-30), 0.0)
        rest = two - guess * one
        for place, value in enumerate(
            (
                along,
                guess,
                total_of(one * rest),
                total_of(rest * rest),
                size,
                largest(two),
                largest(one),
            )
        ):
            found[place].append(value)
    table = share(0, [value for values in found for value in values])()
    total = jnp.sum(table, axis=0, keepdims=True)
    projects, seconds, basis_scale = [], [], jnp.zeros((count, LANES), jnp.float32)
    for s in range(sides):
        guess, cross, rest, size, top_image, top_first = [
            table[:, n * sides + s : n * sides + s + 1] for n in range(1, 7)
        ]
        project = single(total, s) / panels
        off = guess - project
        norm = jnp.sqrt(
            jnp.sum(rest + off * (2.0 * cross + off * size), axis=0, keepdims=True) / panels
            + epsilon
        )
        value = (image[:, lanes[s]] - project * first_ref[:, lanes[s]]) / norm
        basis[:, lanes[s]] = value
        own[:, lanes[s]] = value.astype(jnp.bfloat16)
        bound = (top_image + jnp.abs(project) * top_first) / norm
        basis_scale = basis_scale + jnp.where(iota((count, LANES), 1) == s, bound, 0.0)
        projects.append(project)
        seconds.append(norm)
    mine_scale = jnp.sum(
        jnp.where(iota((count, LANES), 0) == me, basis_scale, 0.0), axis=0, keepdims=True
    )
    every = pl.ds(0, sides * capacity)
    basis_start, basis_recv, basis_send = to_all(1, sent_basis, landed_basis, every)
    image_start, image_recv, image_send = to_all(2, sent_image, landed_image, every)

    def send_basis():
        slot_codes(basis[...], [single(mine_scale, s) for s in range(sides)], sent_basis)
        basis_start()

    operate(1, send_basis)
    scales = [largest(image[:, lanes[s]]) for s in range(sides)]
    slot_codes(image[...], scales, sent_image)
    image_start()
    values = []
    for source in (first_ref, basis):
        for s in range(sides):
            values.append(total_of(source[:, lanes[s]] * image[:, lanes[s]]))
    wait = share(1, values + scales)
    basis_recv()
    returned = home(landed_basis, basis_scale)
    for s in range(sides):
        basis_ref[stride[s], :] = returned[s]
    table = wait()
    total = jnp.sum(table, axis=0, keepdims=True) / panels
    ends = [[single(total, n * sides + s) for s in range(sides)] for n in range(2)]
    for place, found in enumerate((norms, projects, seconds, ends[0], ends[1])):
        line = jnp.zeros((1, LANES), jnp.float32)
        for s in range(sides):
            line = line + jnp.where(lane_row == s, found[s], 0.0)
        entries_ref[place : place + 1] = line[:, :sides]
    kept = iota((count, LANES), 1)
    image_scale = jnp.zeros((count, LANES), jnp.float32)
    for s in range(sides):
        image_scale = image_scale + jnp.where(
            kept == s, table[:, 2 * sides + s : 2 * sides + s + 1], 0.0
        )
    image_recv()
    landed_values = home(landed_image, image_scale)
    for s in range(sides):
        next_ref[stride[s], :] = (
            landed_values[s]
            - ends[0][s] * (side_ref[stride[s], :] / norms[s])
            - ends[1][s] * returned[s]
        )
    basis_send()
    image_send()


def body(
    right_side,
    cluster_of,
    near_rows,
    near_columns,
    near_blocks,
    far_rows,
    far_columns,
    far_rank,
    far_left,
    far_right,
):
    rows = lax.axis_size("row")
    columns = lax.axis_size("col")
    count = rows * columns
    blocks, sides, lanes = right_side.shape
    width = sides * lanes
    capacity = max(TILE, 2 * blocks // count)
    near_groups = near_rows.shape[0] // lanes
    near_blocks = near_blocks.reshape(near_groups, -1, *near_blocks.shape[1:])
    far_left = far_left.reshape(columns, -1, *far_left.shape[1:])
    far_right = far_right.reshape(columns, -1, *far_right.shape[1:])
    halo = blocks // 4
    pairs = columns // 2
    dma = pltpu.SemaphoreType.DMA
    real, half, code = jnp.float32, jnp.bfloat16, jnp.int16
    out_slots = (count, sides * capacity + TILE, lanes)
    code_slots = (count, sides * capacity, lanes)
    hbm = pl.BlockSpec(memory_space=pl.ANY)
    basis, following, entries = pl.pallas_call(
        functools.partial(arnoldi_kernel, rows, columns),
        out_shape=[
            jax.ShapeDtypeStruct((blocks * sides, lanes), real),
            jax.ShapeDtypeStruct((blocks * sides, lanes), real),
            jax.ShapeDtypeStruct((5, sides), real),
        ],
        in_specs=[VMEM] * 7 + [hbm] * 3,
        out_specs=[VMEM] * 3,
        scratch_shapes=[
            pltpu.VMEM((near_groups, 8, lanes), real),
            pltpu.VMEM((columns, 8, lanes), real),
            pltpu.VMEM(out_slots, real),
            pltpu.VMEM(out_slots, real),
            pltpu.VMEM(code_slots, code),
            pltpu.VMEM(code_slots, code),
            pltpu.VMEM(code_slots, code),
            pltpu.VMEM(code_slots, code),
            pltpu.VMEM((blocks, width), real),
            pltpu.VMEM(near_blocks.shape, half),
            pltpu.VMEM(far_left.shape, half),
            pltpu.VMEM(far_right.shape, half),
            pltpu.VMEM((blocks, width), half),
            pltpu.VMEM((blocks, width), real),
            pltpu.VMEM((blocks, width), real),
            pltpu.VMEM((rows, blocks, width), half),
            pltpu.VMEM((blocks + 2 * halo, width), half),
            pltpu.VMEM((halo, width), half),
            pltpu.VMEM((halo, width), half),
            pltpu.VMEM((near_blocks.shape[1], width), real),
            pltpu.VMEM((far_left.shape[1], width), real),
            pltpu.VMEM((pairs, blocks, width), real),
            pltpu.VMEM((pairs, blocks, width), real),
            pltpu.VMEM((pairs, blocks, width), real),
            pltpu.VMEM((pairs, blocks, width), real),
            pltpu.VMEM((pairs, blocks, width), code),
            pltpu.VMEM((pairs, blocks, width), code),
            pltpu.VMEM((pairs, sides * TILE, lanes), real),
            pltpu.VMEM((pairs, sides * TILE, lanes), real),
            pltpu.VMEM((2, TILE, lanes), real),
            pltpu.VMEM((2, count, TILE, lanes), real),
            dma((3, max(columns, near_groups))),
            dma((2, 2)),
            dma((2, 2)),
            dma((2, 2, rows - 1)),
            dma((2, 2, rows - 1)),
            dma((2, pairs)),
            dma((2, pairs)),
            dma((2, pairs)),
            dma((2, pairs)),
            dma((pairs,)),
            dma((pairs,)),
            dma((5,)),
            dma((5,)),
        ],
        compiler_params=pltpu.CompilerParams(
            collective_id=0, has_side_effects=True, vmem_limit_bytes=LIMIT
        ),
    )(
        right_side.reshape(blocks * sides, lanes),
        cluster_of.reshape(1, blocks),
        near_columns.reshape(near_groups, -1),
        near_rows.reshape(near_groups, -1),
        far_columns.reshape(columns, -1),
        far_rows.reshape(columns, -1),
        far_rank.reshape(columns, -1),
        near_blocks,
        far_left,
        far_right,
    )
    shape = (blocks, sides, lanes)
    return (basis.reshape(shape), following.reshape(shape), entries)


def solution(mesh):
    vector = P(("row", "col"), None, None)
    table = P(("row", "col"))
    placed = (vector, table, table, table, vector, table, table, table, vector, vector)
    return jax.shard_map(
        body,
        mesh=mesh,
        in_specs=placed,
        out_specs=(vector, vector, P()),
        check_vma=False,
    )
```

time: 153 us -> 114 us (0.75)
  Pallas kernels: 134 us -> 108 us
  other arithmetic: 7.36 us -> 0 us
  matrix products: 3.44 us -> 0 us
  local copies, waits for them, and re-layouts: 6.71 us -> 4.67 us
    pallas_call x2 -> x1, Pallas kernels: 134 us -> 108 us  [body(): pl.pallas_call(functools.partial(arnoldi_kernel, rows, columns), out_shap...]
    reshape x5 -> x0, local copies, waits for them, and re-layouts: 4.89 us -> none  [the longest x1 1.74 us: body(): second_basis = basis.reshape(blocks, sides, lanes)]
    unnamed x8 -> x3, local copies, waits for them, and re-layouts: 0.76 us -> 4.67 us
    dot_general x2 -> x0, matrix products: 3.44 us -> none  [the longest x1 2.1 us: body(): jnp.dot(to_cluster, arrived[:, :width], precision=HIGH)]
    reduce_sum x4 -> x0, other arithmetic: 2.52 us -> none  [the longest x1 1.2 us: body(): squares = jnp.sum(right_side * right_side, axis=(0, 2))]
where the time goes in v1:
time: 114 us
  Pallas kernels  108 us (95%)
  local copies, waits for them, and re-layouts  4.67 us (4%)
    pallas_call x1, Pallas kernels, body(): pl.pallas_call(functools.partial(arnoldi_kernel, rows, columns), out_shap...  108 us
    unnamed x3, local copies, waits for them, and re-layouts  4.67 us

profile of v1, /device:TPU:0, one launch (start us, length us, event | category | flops | bytes accessed | tf_op | source)
XLA Modules:
  0.0 113.5 jit_solution(2017778313522807873)
XLA Ops:
  0.6 108.2 %shard_map.121 = (f32[512,128]{1,0:T(8,128)}, f32[512,128]{1,0:T(8,128)}, f32[5,4]{1,0:T(8,128)}) custom-call(f32[512,128]{1,0:T(8,128)} %bitcast.15, s32[1,128]{1,0:T(1,128)} %bitcast.23, s32[3,128]{1,0:T(4,128)} %bitcast.21, s32[3,128]{1,0:T(4,128)} %bitcast.22, s32[8,128]{1,0:T(8,128)} %bitcast.18, s32[8,128]{1,0:T(8,128)} %bitcast.19, ...), custom_call_target="tpu_custom_call" | custom-call | tf_op jit(solution)/shard_map/pallas_call | solution.py:705
  108.9 1.3 %copy.13 = f32[5,4]{0,1:T(4,128)} copy(f32[5,4]{1,0:T(8,128)} %get-tuple-element.11) | data formatting | bytes 160
  110.2 1.7 %copy.16 = f32[128,4,128]{2,1,0:T(4,128)} copy(f32[128,4,128]{2,1,0:T(4,128)} %bitcast.17) | data formatting | bytes 524288
  111.9 1.7 %copy.17 = f32[128,4,128]{2,1,0:T(4,128)} copy(f32[128,4,128]{2,1,0:T(4,128)} %bitcast.16) | data formatting | bytes 524288

commit v2 on v1

--- a/solution.py
+++ b/solution.py
@@ -61,83 +61,92 @@
     )
 
 
-def near_group(sides, g, tables_ref, extended, near_ref, near_out, image):
+def corners(one, two):
+    empty = jnp.zeros_like(one)
+    return jnp.concatenate(
+        [jnp.concatenate([one, empty], axis=1), jnp.concatenate([empty, two], axis=1)], axis=0
+    )
+
+
+def near_group(sides, g, near_picked, near_place, near_ref, near_out, image, terms):
     near_count = near_ref.shape[1]
-    reach = extended.shape[0]
-    blocks = image.shape[0]
-    table = tables_ref[g]
-    turned = table.T
-    column = turned[:near_count, 0:1]
-    pick = one_hot(
-        column == lax.broadcasted_iota(jnp.int32, (near_count, reach), 1).astype(jnp.float32)
-    )
-    picked = jnp.dot(pick, extended[...], preferred_element_type=jnp.float32)
-    batch = 8
-    row_id = lax.rem(lax.broadcasted_iota(jnp.int32, (sides * batch, LANES), 0), batch)
-    for j in range(near_count // batch):
-        here = slice(j * batch, (j + 1) * batch)
-        stacked = jnp.concatenate(
-            [picked[here, s * LANES : (s + 1) * LANES] for s in range(sides)], axis=0
-        ).astype(jnp.bfloat16)
+    half = 8
+    both = 2 * half
+    shape = (sides * half, LANES)
+    row_id = lax.rem(lax.broadcasted_iota(jnp.int32, shape, 0), half)
+    for j in range(near_count // both):
+        here = [slice(j * both + n * half, j * both + (n + 1) * half) for n in range(2)]
+        rows = [
+            jnp.concatenate(
+                [near_picked[g, here[n], s * LANES : (s + 1) * LANES] for s in range(sides)],
+                axis=0,
+            ).astype(jnp.bfloat16)
+            for n in range(2)
+        ]
+        weights = jnp.concatenate(
+            [near_ref[g, here[n]].reshape(half * LANES, LANES) for n in range(2)], axis=1
+        )
         product = lax.dot_general(
-            stacked,
-            near_ref[g, here].reshape(batch * LANES, LANES),
+            corners(*rows), weights, (((1,), (1,)), ((), ())), preferred_element_type=jnp.float32
+        )
+        for n in range(2):
+            part = product[n * sides * half : (n + 1) * sides * half]
+            value = part[:, :LANES]
+            for e in range(1, half):
+                value = jnp.where(row_id == e, part[:, e * LANES : (e + 1) * LANES], value)
+            for s in range(sides):
+                near_out[here[n], s * LANES : (s + 1) * LANES] = value[s * half : (s + 1) * half]
+    image[...] += split_dot(near_place[g], near_out[...], terms)
+
+
+def far_group(
+    sides, terms, g, far_picked, far_place, far_ranks, far_left, far_right, far_out
+):
+    far_count, rank = far_left.shape[1:3]
+    half = 16
+    both = 2 * half
+    shape = (sides * half, half * rank)
+    entry = lax.rem(lax.broadcasted_iota(jnp.int32, shape, 0), half)
+    lane = lax.broadcasted_iota(jnp.int32, shape, 1)
+    term = lax.rem(lane, rank).astype(jnp.float32)
+    own_entry = lax.div(lane, rank) == entry
+    kept = []
+    batches = [
+        [slice(j * both + n * half, j * both + (n + 1) * half) for n in range(2)]
+        for j in range(far_count // both)
+    ]
+
+    def weights(factor, here):
+        return jnp.concatenate(
+            [factor[g, part].reshape(half * rank, LANES) for part in here], axis=1
+        )
+
+    for here in batches:
+        rows = [
+            jnp.concatenate(
+                [far_picked[g, part, s * LANES : (s + 1) * LANES] for s in range(sides)], axis=0
+            )
+            for part in here
+        ]
+        product = lax.dot_general(
+            corners(*rows),
+            weights(far_right, here),
             (((1,), (1,)), ((), ())),
             preferred_element_type=jnp.float32,
         )
-        value = jnp.zeros((sides * batch, LANES), jnp.float32)
-        for e in range(batch):
-            value = jnp.where(row_id == e, product[:, e * LANES : (e + 1) * LANES], value)
-        for s in range(sides):
-            near_out[here, s * LANES : (s + 1) * LANES] = value[s * batch : (s + 1) * batch]
-    place = one_hot(
-        table[1:2, :near_count]
-        == lax.broadcasted_iota(jnp.int32, (blocks, near_count), 0).astype(jnp.float32)
-    )
-    image[...] += split_dot(place, near_out[...])
-
-
-def far_group(sides, g, tables_ref, everything, far_left, far_right, far_out):
-    rows, blocks, width = everything.shape
-    far_count, rank = far_left.shape[1:3]
-    table = tables_ref[g]
-    turned = table.T
-    lanes = lax.broadcasted_iota(jnp.int32, (far_count, rows * blocks), 1).astype(jnp.float32)
-    pick = one_hot(turned[:far_count, 0:1] == lanes)
-    picked = jnp.dot(
-        pick, everything[...].reshape(rows * blocks, width), preferred_element_type=jnp.float32
-    )
-    batch = 32
-    shape = (sides * batch, batch * rank)
-    entry = lax.rem(lax.broadcasted_iota(jnp.int32, shape, 0), batch)
-    lane = lax.broadcasted_iota(jnp.int32, shape, 1)
-    term = lax.rem(lane, rank).astype(jnp.float32)
-    own_entry = lax.div(lane, rank) == entry
-    for j in range(far_count // batch):
-        here = slice(j * batch, (j + 1) * batch)
-        stacked = jnp.concatenate(
-            [picked[here, s * LANES : (s + 1) * LANES] for s in range(sides)], axis=0
-        ).astype(jnp.bfloat16)
-        product = lax.dot_general(
-            stacked,
-            far_right[g, here].reshape(batch * rank, LANES),
-            (((1,), (1,)), ((), ())),
-            preferred_element_type=jnp.float32,
-        )
-        ranks = jnp.concatenate([turned[here, 2:3]] * sides, axis=0)
-        coefficients = jnp.where(own_entry & (term < ranks), product, 0.0).astype(jnp.bfloat16)
-        value = jnp.dot(
-            coefficients,
-            far_left[g, here].reshape(batch * rank, LANES),
-            preferred_element_type=jnp.float32,
-        )
-        for s in range(sides):
-            far_out[here, s * LANES : (s + 1) * LANES] = value[s * batch : (s + 1) * batch]
-    place = one_hot(
-        table[1:2, :far_count]
-        == lax.broadcasted_iota(jnp.int32, (blocks, far_count), 0).astype(jnp.float32)
-    )
-    return split_dot(place, far_out[...])
+        parts = []
+        for n in range(2):
+            ranks = jnp.concatenate([far_ranks[g, here[n], 0:1]] * sides, axis=0)
+            part = product[n * sides * half : (n + 1) * sides * half]
+            parts.append(jnp.where(own_entry & (term < ranks), part, 0.0).astype(jnp.bfloat16))
+        kept.append(jnp.concatenate(parts, axis=0))
+    for here, coefficients in zip(batches, kept):
+        value = jnp.dot(coefficients, weights(far_left, here), preferred_element_type=jnp.float32)
+        for n in range(2):
+            part = value[n * sides * half : (n + 1) * sides * half, n * LANES : (n + 1) * LANES]
+            for s in range(sides):
+                far_out[here[n], s * LANES : (s + 1) * LANES] = part[s * half : (s + 1) * half]
+    return split_dot(far_place[g], far_out[...], terms)
 
 
 def iota(shape, dimension):
@@ -176,10 +185,18 @@
     far_left_hbm,
     far_right_hbm,
     basis_ref,
+    basis_rest_ref,
     next_ref,
+    next_rest_ref,
     entries_ref,
-    near_tables,
-    far_tables,
+    tables,
+    near_pick,
+    near_place,
+    near_picked,
+    far_pick,
+    far_place,
+    far_ranks,
+    far_picked,
     sent,
     landed,
     sent_basis,
@@ -284,8 +301,12 @@
 
         def copy(peer, here):
             return pltpu.make_async_remote_copy(
-                src_ref=mine.at[n] if here is not None else parts.at[n, pl.ds(0, count - 1)],
-                dst_ref=parts.at[n, here if here is not None else pl.ds(0, count - 1)],
+                src_ref=(
+                    parts.at[n, pl.ds(0, count - 1), pl.ds(0, 1)]
+                    if here is None
+                    else mine.at[n, pl.ds(0, 1)]
+                ),
+                dst_ref=parts.at[n, pl.ds(0, count - 1) if here is None else here, pl.ds(0, 1)],
                 send_sem=all_send.at[3 + n],
                 recv_sem=all_recv.at[3 + n],
                 device_id=coordinates(peer, columns),
@@ -341,20 +362,32 @@
     else:
         sent[:, top:, :] = extra.reshape(count, capacity, LANES)[:, :TILE]
     enter(me, rows, columns)
-    out_start, out_recv, out_send = to_all(0, sent, landed, pl.ds(0, top + TILE))
+    out_start, out_recv, out_send = to_all(0, sent, landed, pl.ds(0, top + 1))
     out_start()
 
-    near_tables[...] = jnp.zeros(near_tables.shape, jnp.float32)
+    near_count, far_count = near_ref.shape[1], far_left.shape[1]
+
+    def turn(g, *sources):
+        tables[g] = jnp.zeros(tables.shape[1:], jnp.float32)
+        for spot, source in enumerate(sources):
+            tables[g, spot : spot + 1, : source.shape[1]] = source.astype(jnp.float32)
+        return tables[g].T
+
+    def matches(column, many):
+        return one_hot(column == iota((column.shape[0], many), 1).astype(jnp.float32))
+
+    def places(row_of):
+        return one_hot(iota((blocks, row_of.shape[1]), 0) == row_of)
+
     for g in range(near_groups):
-        for spot, source in enumerate((near_columns_ref, near_rows_ref)):
-            near_tables[g, spot : spot + 1] = source[g : g + 1].astype(jnp.float32)
-    far_tables[...] = jnp.zeros(far_tables.shape, jnp.float32)
+        column_of = turn(g, near_columns_ref[g : g + 1])
+        near_pick[g] = matches(column_of[:near_count, 0:1], extended.shape[0])
+        near_place[g] = places(near_rows_ref[g : g + 1])
     for g in range(groups):
-        for spot, source in enumerate((far_columns_ref, far_rows_ref, far_rank_ref)):
-            value = source[g : g + 1]
-            if source is far_rows_ref:
-                value = value - g * blocks
-            far_tables[g, spot : spot + 1, : source.shape[1]] = value.astype(jnp.float32)
+        column_of = turn(near_groups + g, far_columns_ref[g : g + 1], far_rank_ref[g : g + 1])
+        far_pick[g] = matches(column_of[:far_count, 0:1], rows * blocks)
+        far_ranks[g] = jnp.broadcast_to(column_of[:far_count, 1:2], far_ranks.shape[1:])
+        far_place[g] = places(far_rows_ref[g : g + 1] - g * blocks)
 
     out_recv()
     table = landed[:, top, :]
@@ -404,62 +437,64 @@
         def inside(index):
             return (index >= 0) & (index < rows)
 
-        def hop(way, distance, slot):
+        def hop(way, distance, source):
             sign = 1 - 2 * way
+            reach = 2 if distance == 2 else 1
             return remote(
-                everything.at[slot],
-                everything.at[slot],
+                everything.at[source],
+                everything.at[source],
                 spread_send.at[a, way],
                 spread_recv.at[a, way],
-                distance,
-                (lax.rem(row + sign + rows, rows), column),
+                distance - 1,
+                (lax.rem(row + sign * reach + 2 * rows, rows), column),
             )
 
-        def relay(distance):
+        def arrive(distance):
+            for way in range(2):
+                source = row - (1 - 2 * way) * distance
+
+                @pl.when(inside(source))
+                def _(way=way, source=source):
+                    hop(way, distance, source).wait_recv()
+
+        def each_hop(distance, act):
             for way in range(2):
                 sign = 1 - 2 * way
-                source = row - sign * distance
-                if distance > 0:
-
-                    @pl.when(inside(source))
-                    def _(way=way, source=source):
-                        hop(way, distance - 1, source).wait_recv()
-
-                if distance < rows - 1:
-
-                    @pl.when(inside(source) & inside(row + sign))
-                    def _(way=way, source=source):
-                        hop(way, distance, source).start()
-
-        relay(0)
+                held_at = 0 if distance < 3 else distance - 1
+                source = row - sign * held_at
+                there = row + sign * (2 if distance == 2 else 1)
+
+                @pl.when(inside(source) & inside(there))
+                def _(way=way, source=source):
+                    act(hop(way, distance, source))
+
+        each_hop(1, lambda copy: copy.start())
+        if rows > 2:
+            each_hop(2, lambda copy: copy.start())
         image[...] = 0.5 * own[...].astype(jnp.float32)
         extended[halo : halo + blocks] = own[...]
         for copy in halos:
             copy.wait()
         extended[0:halo] = left[...]
         extended[halo + blocks :] = right[...]
+        for g in range(near_groups):
+            near_picked[g] = jnp.dot(
+                near_pick[g], extended[...], preferred_element_type=jnp.float32
+            )
 
         @pl.loop(0, near_groups)
         def _(g):
             if a == 0:
                 load(0, g).wait()
-            near_group(sides, g, near_tables, extended, near_ref, near_out, image)
-            for distance in range(1, rows - 1):
-
-                @pl.when(g == distance * near_groups // (rows - 1))
-                def _(distance=distance):
-                    relay(distance)
-
-        relay(rows - 1)
-        for way in range(2):
-            sign = 1 - 2 * way
-            for distance in range(rows - 1):
-                source = row - sign * distance
-
-                @pl.when(inside(source) & inside(row + sign))
-                def _(way=way, source=source, distance=distance):
-                    hop(way, distance, source).wait_send()
-
+            near_group(sides, g, near_picked, near_place, near_ref, near_out, image, 3 - a)
+
+        for distance in range(3, rows):
+            arrive(distance - 1)
+            each_hop(distance, lambda copy: copy.start())
+        for distance in sorted({1, rows - 1}):
+            arrive(distance)
+        for distance in range(1, rows):
+            each_hop(distance, lambda copy: copy.wait_send())
         between()
         if a == 0:
             for kind in (1, 2):
@@ -468,11 +503,20 @@
                 def _(g, kind=kind):
                     load(kind, g).wait()
 
+        for g in range(groups):
+            far_picked[g] = jnp.dot(
+                far_pick[g],
+                everything[...].reshape(rows * blocks, width),
+                preferred_element_type=jnp.float32,
+            ).astype(jnp.bfloat16)
+
         far = functools.partial(
             far_group,
             sides,
-            tables_ref=far_tables,
-            everything=everything,
+            3 - a,
+            far_picked=far_picked,
+            far_place=far_place,
+            far_ranks=far_ranks,
             far_left=far_left,
             far_right=far_right,
             far_out=far_out,
@@ -516,9 +560,13 @@
         @pl.loop(1, pairs + 1)
         def _(i):
             q = lax.rem(chip + i, pairs)
+            to_partner[q] = far(2 * q + 1 - core)
+            pair_copy(i - 1, q).start()
+
+        @pl.loop(1, pairs + 1)
+        def _(i):
+            q = lax.rem(chip + i, pairs)
             k = i - 1
-            to_partner[q] = far(2 * q + 1 - core)
-            pair_copy(k, q).start()
             to_chips[q] = far(2 * q + core)
             pair_copy(k, q).wait_recv()
             to_chips[q] = to_chips[q] + from_partner[q]
@@ -580,8 +628,15 @@
             both = decode(buffer[:, s * capacity : (s + 2) * capacity, :])
             for side in (s, s + 1):
                 code = both[:, (side - s) * capacity : (side - s + 1) * capacity]
-                value = split_dot(to_own, code.reshape(slots, LANES), 2)
-                values.append(value * (own_scales[:, side : side + 1] * (1.0 / TOP)))
+                code = code.reshape(slots, LANES)
+                high = code.astype(jnp.bfloat16)
+                scale = own_scales[:, side : side + 1] * (1.0 / TOP)
+                values.append(
+                    (
+                        split_dot(to_own, high, 1) * scale,
+                        split_dot(to_own, code - high.astype(jnp.float32), 1) * scale,
+                    )
+                )
         return values
 
     operate(0, lambda: None)
@@ -646,15 +701,15 @@
     basis_recv()
     returned = home(landed_basis, basis_scale)
     for s in range(sides):
-        basis_ref[stride[s], :] = returned[s]
+        basis_ref[stride[s], :], basis_rest_ref[stride[s], :] = returned[s]
     table = wait()
     total = jnp.sum(table, axis=0, keepdims=True) / panels
     ends = [[single(total, n * sides + s) for s in range(sides)] for n in range(2)]
-    for place, found in enumerate((norms, projects, seconds, ends[0], ends[1])):
+    for s in range(sides):
         line = jnp.zeros((1, LANES), jnp.float32)
-        for s in range(sides):
-            line = line + jnp.where(lane_row == s, found[s], 0.0)
-        entries_ref[place : place + 1] = line[:, :sides]
+        for place, found in enumerate((norms, projects, seconds, ends[0], ends[1])):
+            line = line + jnp.where(lane_row == place, found[s], 0.0)
+        entries_ref[s : s + 1] = line[:, : entries_ref.shape[1]]
     kept = iota((count, LANES), 1)
     image_scale = jnp.zeros((count, LANES), jnp.float32)
     for s in range(sides):
@@ -664,11 +719,9 @@
     image_recv()
     landed_values = home(landed_image, image_scale)
     for s in range(sides):
-        next_ref[stride[s], :] = (
-            landed_values[s]
-            - ends[0][s] * (side_ref[stride[s], :] / norms[s])
-            - ends[1][s] * returned[s]
-        )
+        high, rest = landed_values[s]
+        next_ref[stride[s], :] = high + rest - ends[0][s] * (side_ref[stride[s], :] / norms[s])
+        next_rest_ref[stride[s], :] = ends[1][s] * (returned[s][0] + returned[s][1])
     basis_send()
     image_send()
 
@@ -695,6 +748,7 @@
     near_blocks = near_blocks.reshape(near_groups, -1, *near_blocks.shape[1:])
     far_left = far_left.reshape(columns, -1, *far_left.shape[1:])
     far_right = far_right.reshape(columns, -1, *far_right.shape[1:])
+    near_count, far_count = near_blocks.shape[1], far_left.shape[1]
     halo = blocks // 4
     pairs = columns // 2
     dma = pltpu.SemaphoreType.DMA
@@ -702,18 +756,23 @@
     out_slots = (count, sides * capacity + TILE, lanes)
     code_slots = (count, sides * capacity, lanes)
     hbm = pl.BlockSpec(memory_space=pl.ANY)
-    basis, following, entries = pl.pallas_call(
+    basis, basis_rest, following, following_rest, entries = pl.pallas_call(
         functools.partial(arnoldi_kernel, rows, columns),
         out_shape=[
-            jax.ShapeDtypeStruct((blocks * sides, lanes), real),
-            jax.ShapeDtypeStruct((blocks * sides, lanes), real),
-            jax.ShapeDtypeStruct((5, sides), real),
+            *[jax.ShapeDtypeStruct((blocks * sides, lanes), real)] * 4,
+            jax.ShapeDtypeStruct((sides, 5), real),
         ],
         in_specs=[VMEM] * 7 + [hbm] * 3,
-        out_specs=[VMEM] * 3,
+        out_specs=[VMEM] * 5,
         scratch_shapes=[
-            pltpu.VMEM((near_groups, 8, lanes), real),
-            pltpu.VMEM((columns, 8, lanes), real),
+            pltpu.VMEM((near_groups + columns, TILE, lanes), real),
+            pltpu.VMEM((near_groups, near_count, blocks + 2 * halo), half),
+            pltpu.VMEM((near_groups, blocks, near_count), half),
+            pltpu.VMEM((near_groups, near_count, width), real),
+            pltpu.VMEM((columns, far_count, rows * blocks), half),
+            pltpu.VMEM((columns, blocks, far_count), half),
+            pltpu.VMEM((columns, far_count, lanes), real),
+            pltpu.VMEM((columns, far_count, width), half),
             pltpu.VMEM(out_slots, real),
             pltpu.VMEM(out_slots, real),
             pltpu.VMEM(code_slots, code),
@@ -773,7 +832,11 @@
         far_right,
     )
     shape = (blocks, sides, lanes)
-    return (basis.reshape(shape), following.reshape(shape), entries)
+    return (
+        (basis + basis_rest).reshape(shape),
+        (following - following_rest).reshape(shape),
+        entries.T,
+    )
 
 
 def solution(mesh):

time: 114 us -> 105 us (0.921)
  Pallas kernels: 108 us -> 99 us
  other arithmetic: 0 us -> 3.52 us
  local copies, waits for them, and re-layouts: 4.67 us -> 1.26 us
    pallas_call x1, Pallas kernels: 108 us -> 99 us  [body(): pl.pallas_call(functools.partial(arnoldi_kernel, rows, columns), out_shap...]
    unnamed x3 -> x1, local copies, waits for them, and re-layouts: 4.67 us -> 1.26 us
    add x0 -> x1, other arithmetic: none -> 1.76 us  [body(): basis + basis_rest]
    sub x0 -> x1, other arithmetic: none -> 1.76 us  [body(): following - following_rest]
where the time goes in v2:
time: 105 us; the launch traced here: 104 us
  Pallas kernels  99 us (94%)
  other arithmetic  3.52 us (3%)
  local copies, waits for them, and re-layouts  1.26 us (1%)
    pallas_call x1, Pallas kernels, body(): pl.pallas_call(functools.partial(arnoldi_kernel, rows, columns), out_shap...  99 us

profile of v2, /device:TPU:0, one launch (start us, length us, event | category | flops | bytes accessed | tf_op | source)
XLA Modules:
  0.0 104.4 jit_solution(12710500996766708215)
XLA Ops:
  0.6 99.0 %shard_map.121 = (f32[512,128]{1,0:T(8,128)}, f32[512,128]{1,0:T(8,128)}, f32[512,128]{1,0:T(8,128)}, f32[512,128]{1,0:T(8,128)}, f32[4,5]{1,0:T(4,128)}) custom-call(f32[512,128]{1,0:T(8,128)} %bitcast.16, s32[1,128]{1,0:T(1,128)} %bitcast.25, s32[3,128]{1,0:T(4,128)} %bitcast.23, s32[3,128]{1,0:T(4,128)} %bitcast.24, s32[8,128]{1,0:T(8,128)} %bitcast.19, ...), custom_call_target="tpu_custom_call" | custom-call | tf_op jit(solution)/shard_map/pallas_call | solution.py:759
  99.6 1.8 %add.3 = f32[512,128]{1,0:T(8,128)} add(f32[512,128]{1,0:T(8,128)} %get-tuple-element.8, f32[512,128]{1,0:T(8,128)} %get-tuple-element.9) | non-fusion elementwise | flops 65536 | bytes 786432 | tf_op jit(solution)/shard_map/add | solution.py:836
  101.4 1.8 %sub.3 = f32[512,128]{1,0:T(8,128)} subtract(f32[512,128]{1,0:T(8,128)} %get-tuple-element.10, f32[512,128]{1,0:T(8,128)} %get-tuple-element.11) | non-fusion elementwise | flops 65536 | bytes 786432 | tf_op jit(solution)/shard_map/sub | solution.py:837
  103.1 1.3 %copy.14 = f32[5,4]{0,1:T(4,128)} copy(f32[5,4]{0,1:T(4,128)} %bitcast.22) | data formatting | bytes 160

commit v3 on v2

--- a/solution.py
+++ b/solution.py
@@ -14,13 +14,15 @@
 LIMIT = 56 * 2**20
 TILE = 8
 TOP = 32767.0
+WIDE = 8388607.0
+BYTE = 256.0
 
 
 def coordinates(index, column_count):
     return (lax.div(index, column_count), lax.rem(index, column_count))
 
 
-def enter(me, rows, columns):
+def greet(me, rows, columns):
     count = rows * columns
     barrier = pltpu.get_barrier_semaphore()
 
@@ -33,7 +35,7 @@
             device_id_type=MESH,
         )
 
-    pl.semaphore_wait(barrier, count - 1)
+    return functools.partial(pl.semaphore_wait, barrier, count - 1)
 
 
 def split_dot(picker, value, terms=3):
@@ -153,8 +155,11 @@
     return lax.broadcasted_iota(jnp.int32, shape, dimension)
 
 
-def encode(value, scale):
-    code = jnp.floor(jnp.clip(value * (TOP / scale), -TOP, TOP) + 0.5)
+def to_code(value, scale, top):
+    return jnp.floor(jnp.clip(value * (top / scale), -top, top) + 0.5)
+
+
+def narrow(code):
     return code.astype(jnp.int32).astype(jnp.int16)
 
 
@@ -219,7 +224,8 @@
     to_partner,
     from_partner,
     to_chips,
-    from_chips,
+    wide_to,
+    wide_from,
     code_to,
     code_from,
     scale_to,
@@ -256,6 +262,8 @@
     capacity = (sent.shape[1] - TILE) // sides
     slots = count * capacity
     lane_row = iota((1, LANES), 1)
+    code_to, code_from = (wide_to, code_to), (wide_from, code_from)
+    entered = greet(me, rows, columns)
 
     def load(kind, g):
         source, target = (
@@ -361,7 +369,7 @@
         sent[:, top:, :] = extra.reshape(count, TILE, LANES)
     else:
         sent[:, top:, :] = extra.reshape(count, capacity, LANES)[:, :TILE]
-    enter(me, rows, columns)
+    entered()
     out_start, out_recv, out_send = to_all(0, sent, landed, pl.ds(0, top + 1))
     out_start()
 
@@ -534,68 +542,84 @@
 
         def chip_copies(k, q, here):
             device = (row, 2 * q + core)
-            if a == 0:
-                return [
-                    remote(
-                        to_chips.at[q],
-                        from_chips.at[here],
-                        chip_send.at[a],
-                        chip_recv.at[a],
-                        k,
-                        device,
-                    )
-                ]
             return [
                 remote(
-                    code_to.at[q],
-                    code_from.at[here],
+                    code_to[a].at[q],
+                    code_from[a].at[here],
                     chip_send.at[a],
                     chip_recv.at[a],
                     k,
                     device,
                 ),
-                remote(scale_to.at[q], scale_from.at[here], scale_send, scale_recv, k, device),
+                remote(
+                    scale_to.at[a, q],
+                    scale_from.at[a, here],
+                    scale_send.at[a],
+                    scale_recv.at[a],
+                    k,
+                    device,
+                ),
             ]
 
-        @pl.loop(1, pairs + 1)
-        def _(i):
-            q = lax.rem(chip + i, pairs)
-            to_partner[q] = far(2 * q + 1 - core)
-            pair_copy(i - 1, q).start()
-
-        @pl.loop(1, pairs + 1)
-        def _(i):
-            q = lax.rem(chip + i, pairs)
-            k = i - 1
-            to_chips[q] = far(2 * q + core)
-            pair_copy(k, q).wait_recv()
-            to_chips[q] = to_chips[q] + from_partner[q]
-
-            @pl.when(i < pairs)
+        top_code = WIDE if a == 0 else TOP
+
+        def pack(source, q):
+            lows = []
+            for s in range(sides):
+                value = source[q, :, lanes[s]]
+                scale = jnp.maximum(jnp.max(jnp.abs(value), axis=0, keepdims=True), 1e-30)
+                scale_to[a, q, s * TILE : (s + 1) * TILE] = jnp.broadcast_to(scale, (TILE, LANES))
+                code = to_code(value, scale, top_code)
+                if a == 0:
+                    high = jnp.floor(code * (1.0 / BYTE))
+                    lows.append(code - high * BYTE)
+                    code = high
+                code_to[a][q, :, lanes[s]] = narrow(code)
+            for n in range(len(lows) // 2):
+                code = lows[2 * n] * BYTE + (lows[2 * n + 1] - BYTE * BYTE / 2)
+                code_to[a][q, :, width + n * LANES : width + (n + 1) * LANES] = narrow(code)
+
+        def unpack(q):
+            codes = [decode(code_from[a][q, :, lanes[s]]) for s in range(sides)]
+            if a == 0:
+                for n in range(sides // 2):
+                    both = decode(code_from[a][q, :, width + n * LANES : width + (n + 1) * LANES])
+                    both = both + BYTE * BYTE / 2
+                    high = jnp.floor(both * (1.0 / BYTE))
+                    codes[2 * n] = codes[2 * n] * BYTE + high
+                    codes[2 * n + 1] = codes[2 * n + 1] * BYTE + (both - high * BYTE)
+            for s in range(sides):
+                scale = scale_from[a, q, s * TILE : s * TILE + 1] * (1.0 / top_code)
+                image[:, lanes[s]] += codes[s] * scale
+
+        @pl.loop(1, pairs + 2)
+        def _(t):
+            @pl.when(t <= pairs)
             def _():
-                if a == 1:
-                    for s in range(sides):
-                        value = to_chips[q, :, lanes[s]]
-                        scale = jnp.max(jnp.abs(value), axis=0, keepdims=True)
-                        scale = jnp.maximum(scale, 1e-30)
-                        scale_to[q, s * TILE : (s + 1) * TILE] = jnp.broadcast_to(
-                            scale, (TILE, LANES)
-                        )
-                        code_to[q, :, lanes[s]] = encode(value, scale)
-                for copy in chip_copies(k, q, chip):
-                    copy.start()
+                q = lax.rem(chip + t, pairs)
+                to_partner[q] = far(2 * q + 1 - core)
+                pair_copy(t - 1, q).start()
+
+            @pl.when(t > 1)
+            def _():
+                i = t - 1
+                q = lax.rem(chip + i, pairs)
+                to_chips[q] = far(2 * q + core)
+                pair_copy(i - 1, q).wait_recv()
+                to_chips[q] = to_chips[q] + from_partner[q]
+
+                @pl.when(i < pairs)
+                def _():
+                    pack(to_chips, q)
+                    for copy in chip_copies(i - 1, q, chip):
+                        copy.start()
 
         image[...] += to_chips[chip]
         for i in range(1, pairs):
             source = lax.rem(chip + pairs - i, pairs)
             for copy in chip_copies(i - 1, source, source):
                 copy.wait_recv()
-            if a == 0:
-                image[...] += from_chips[source]
-            else:
-                for s in range(sides):
-                    scale = scale_from[source, s * TILE : s * TILE + 1] * (1.0 / TOP)
-                    image[:, lanes[s]] += decode(code_from[source, :, lanes[s]]) * scale
+            unpack(source)
         for i in range(1, pairs + 1):
             q = lax.rem(chip + i, pairs)
             pair_copy(i - 1, q).wait_send()
@@ -607,14 +631,10 @@
         for s in range(0, sides, 2):
             codes = []
             for side in (s, s + 1):
-                code = jnp.floor(
-                    jnp.clip(value[:, lanes[side]] * (TOP / scales[side]), -TOP, TOP) + 0.5
-                )
+                code = to_code(value[:, lanes[side]], scales[side], TOP)
                 codes.append(split_dot(to_mesh, code, 2).reshape(count, capacity, LANES))
             both = jnp.concatenate(codes, axis=1)
-            buffer[:, s * capacity : (s + 2) * capacity, :] = both.astype(jnp.int32).astype(
-                jnp.int16
-            )
+            buffer[:, s * capacity : (s + 2) * capacity, :] = narrow(both)
 
     to_own = one_hot(
         turned_target[:, 0:1] * capacity + rank_column == iota((blocks, slots), 1)
@@ -795,11 +815,12 @@
             pltpu.VMEM((pairs, blocks, width), real),
             pltpu.VMEM((pairs, blocks, width), real),
             pltpu.VMEM((pairs, blocks, width), real),
-            pltpu.VMEM((pairs, blocks, width), real),
+            pltpu.VMEM((pairs, blocks, 3 * width // 2), code),
+            pltpu.VMEM((pairs, blocks, 3 * width // 2), code),
             pltpu.VMEM((pairs, blocks, width), code),
             pltpu.VMEM((pairs, blocks, width), code),
-            pltpu.VMEM((pairs, sides * TILE, lanes), real),
-            pltpu.VMEM((pairs, sides * TILE, lanes), real),
+            pltpu.VMEM((2, pairs, sides * TILE, lanes), real),
+            pltpu.VMEM((2, pairs, sides * TILE, lanes), real),
             pltpu.VMEM((2, TILE, lanes), real),
             pltpu.VMEM((2, count, TILE, lanes), real),
             dma((3, max(columns, near_groups))),
@@ -811,8 +832,8 @@
             dma((2, pairs)),
             dma((2, pairs)),
             dma((2, pairs)),
-            dma((pairs,)),
-            dma((pairs,)),
+            dma((2, pairs)),
+            dma((2, pairs)),
             dma((5,)),
             dma((5,)),
         ],

time: 105 us -> 102 us (0.971)
  Pallas kernels: 99 us -> 96.2 us
    pallas_call x1, Pallas kernels: 99 us -> 96.2 us  [body(): pl.pallas_call(functools.partial(arnoldi_kernel, rows, columns), out_shap...]
where the time goes in v3:
time: 102 us
  Pallas kernels  96.2 us (94%)
  other arithmetic  3.52 us (3%)
  local copies, waits for them, and re-layouts  1.26 us (1%)
    pallas_call x1, Pallas kernels, body(): pl.pallas_call(functools.partial(arnoldi_kernel, rows, columns), out_shap...  96.2 us

profile of v3, /device:TPU:0, one launch (start us, length us, event | category | flops | bytes accessed | tf_op | source)
XLA Modules:
  0.0 101.6 jit_solution(7795207400735863735)
XLA Ops:
  0.6 96.2 %shard_map.121 = (f32[512,128]{1,0:T(8,128)}, f32[512,128]{1,0:T(8,128)}, f32[512,128]{1,0:T(8,128)}, f32[512,128]{1,0:T(8,128)}, f32[4,5]{1,0:T(4,128)}) custom-call(f32[512,128]{1,0:T(8,128)} %bitcast.16, s32[1,128]{1,0:T(1,128)} %bitcast.25, s32[3,128]{1,0:T(4,128)} %bitcast.23, s32[3,128]{1,0:T(4,128)} %bitcast.24, s32[8,128]{1,0:T(8,128)} %bitcast.19, ...), custom_call_target="tpu_custom_call" | custom-call | tf_op jit(solution)/shard_map/pallas_call | solution.py:779
  96.8 1.8 %add.3 = f32[512,128]{1,0:T(8,128)} add(f32[512,128]{1,0:T(8,128)} %get-tuple-element.8, f32[512,128]{1,0:T(8,128)} %get-tuple-element.9) | non-fusion elementwise | flops 65536 | bytes 786432 | tf_op jit(solution)/shard_map/add | solution.py:857
  98.6 1.8 %sub.3 = f32[512,128]{1,0:T(8,128)} subtract(f32[512,128]{1,0:T(8,128)} %get-tuple-element.10, f32[512,128]{1,0:T(8,128)} %get-tuple-element.11) | non-fusion elementwise | flops 65536 | bytes 786432 | tf_op jit(solution)/shard_map/sub | solution.py:858
  100.3 1.3 %copy.14 = f32[5,4]{0,1:T(4,128)} copy(f32[5,4]{0,1:T(4,128)} %bitcast.22) | data formatting | bytes 160

commit v4 on v3

--- a/solution.py
+++ b/solution.py
@@ -16,6 +16,7 @@
 TOP = 32767.0
 WIDE = 8388607.0
 BYTE = 256.0
+HALVES = 2
 
 
 def coordinates(index, column_count):
@@ -39,13 +40,14 @@
 
 
 def split_dot(picker, value, terms=3):
-    total = None
+    parts = []
     for _ in range(terms):
-        part = value.astype(jnp.bfloat16)
-        value = value - part.astype(jnp.float32)
-        product = jnp.dot(picker, part, preferred_element_type=jnp.float32)
-        total = product if total is None else total + product
-    return total
+        parts.append(value.astype(jnp.bfloat16))
+        value = value - parts[-1].astype(jnp.float32)
+    dot = functools.partial(jnp.dot, preferred_element_type=jnp.float32)
+    if picker.shape[1] % LANES == 0:
+        return dot(jnp.concatenate([picker] * terms, axis=1), jnp.concatenate(parts, axis=0))
+    return sum(dot(picker, part) for part in parts)
 
 
 def one_hot(condition):
@@ -102,7 +104,7 @@
 
 
 def far_group(
-    sides, terms, g, far_picked, far_place, far_ranks, far_left, far_right, far_out
+    sides, terms, chosen, far_picked, far_place, far_ranks, far_left, far_right, far_out
 ):
     far_count, rank = far_left.shape[1:3]
     half = 16
@@ -114,16 +116,17 @@
     own_entry = lax.div(lane, rank) == entry
     kept = []
     batches = [
-        [slice(j * both + n * half, j * both + (n + 1) * half) for n in range(2)]
+        (n, g, [slice(j * both + m * half, j * both + (m + 1) * half) for m in range(2)])
+        for n, g in enumerate(chosen)
         for j in range(far_count // both)
     ]
 
-    def weights(factor, here):
+    def weights(factor, g, here):
         return jnp.concatenate(
             [factor[g, part].reshape(half * rank, LANES) for part in here], axis=1
         )
 
-    for here in batches:
+    for _, g, here in batches:
         rows = [
             jnp.concatenate(
                 [far_picked[g, part, s * LANES : (s + 1) * LANES] for s in range(sides)], axis=0
@@ -132,23 +135,25 @@
         ]
         product = lax.dot_general(
             corners(*rows),
-            weights(far_right, here),
+            weights(far_right, g, here),
             (((1,), (1,)), ((), ())),
             preferred_element_type=jnp.float32,
         )
         parts = []
-        for n in range(2):
-            ranks = jnp.concatenate([far_ranks[g, here[n], 0:1]] * sides, axis=0)
-            part = product[n * sides * half : (n + 1) * sides * half]
+        for m in range(2):
+            ranks = jnp.concatenate([far_ranks[g, here[m], 0:1]] * sides, axis=0)
+            part = product[m * sides * half : (m + 1) * sides * half]
             parts.append(jnp.where(own_entry & (term < ranks), part, 0.0).astype(jnp.bfloat16))
         kept.append(jnp.concatenate(parts, axis=0))
-    for here, coefficients in zip(batches, kept):
-        value = jnp.dot(coefficients, weights(far_left, here), preferred_element_type=jnp.float32)
-        for n in range(2):
-            part = value[n * sides * half : (n + 1) * sides * half, n * LANES : (n + 1) * LANES]
+    for (n, g, here), coefficients in zip(batches, kept):
+        value = jnp.dot(
+            coefficients, weights(far_left, g, here), preferred_element_type=jnp.float32
+        )
+        for m in range(2):
+            part = value[m * sides * half : (m + 1) * sides * half, m * LANES : (m + 1) * LANES]
             for s in range(sides):
-                far_out[here[n], s * LANES : (s + 1) * LANES] = part[s * half : (s + 1) * half]
-    return split_dot(far_place[g], far_out[...], terms)
+                far_out[n, here[m], s * LANES : (s + 1) * LANES] = part[s * half : (s + 1) * half]
+    return [split_dot(far_place[g], far_out[n], terms) for n, g in enumerate(chosen)]
 
 
 def iota(shape, dimension):
@@ -251,7 +256,7 @@
     me = row * columns + column
     blocks, width = first_ref.shape
     sides = width // LANES
-    halo = left.shape[0]
+    halo = left.shape[1]
     groups = far_left.shape[0]
     near_groups = near_ref.shape[0]
     pairs = columns // 2
@@ -262,6 +267,7 @@
     capacity = (sent.shape[1] - TILE) // sides
     slots = count * capacity
     lane_row = iota((1, LANES), 1)
+    some = sides // HALVES
     code_to, code_from = (wide_to, code_to), (wide_from, code_from)
     entered = greet(me, rows, columns)
 
@@ -421,51 +427,55 @@
         arrived = landed[:, s * capacity : (s + 1) * capacity, :].reshape(slots, LANES)
         value = split_dot(to_cluster, arrived) / norms[s]
         first_ref[:, lanes[s]] = value
-        own[:, lanes[s]] = value.astype(jnp.bfloat16)
+        own[s // some, :, lanes[s % some]] = value.astype(jnp.bfloat16)
     out_send()
 
-    def operate(a, between):
+    part_width = width // HALVES
+    parts_of = [slice(h * part_width, (h + 1) * part_width) for h in range(HALVES)]
+
+    def operate(a, prepare, between):
         after = coordinates(lax.rem(me + 1, count), columns)
         before = coordinates(lax.rem(me + count - 1, count), columns)
         halos = [
             remote(
-                own.at[pl.ds(blocks - halo, halo)],
+                own.at[:, pl.ds(blocks - halo, halo)],
                 left,
                 halo_send.at[a],
                 halo_recv.at[a],
                 0,
                 after,
             ),
-            remote(own.at[pl.ds(0, halo)], right, halo_send.at[a], halo_recv.at[a], 1, before),
+            remote(own.at[:, pl.ds(0, halo)], right, halo_send.at[a], halo_recv.at[a], 1, before),
         ]
         for copy in halos:
             copy.start()
-        everything[row] = own[...]
+        for h in range(HALVES):
+            everything[h, row] = own[h]
 
         def inside(index):
             return (index >= 0) & (index < rows)
 
-        def hop(way, distance, source):
+        def hop(h, way, distance, source):
             sign = 1 - 2 * way
             reach = 2 if distance == 2 else 1
             return remote(
-                everything.at[source],
-                everything.at[source],
-                spread_send.at[a, way],
-                spread_recv.at[a, way],
+                everything.at[h, source],
+                everything.at[h, source],
+                spread_send.at[a, h, way],
+                spread_recv.at[a, h, way],
                 distance - 1,
                 (lax.rem(row + sign * reach + 2 * rows, rows), column),
             )
 
-        def arrive(distance):
+        def arrive(h, distance):
             for way in range(2):
                 source = row - (1 - 2 * way) * distance
 
                 @pl.when(inside(source))
                 def _(way=way, source=source):
-                    hop(way, distance, source).wait_recv()
-
-        def each_hop(distance, act):
+                    hop(h, way, distance, source).wait_recv()
+
+        def each_hop(h, distance, act):
             for way in range(2):
                 sign = 1 - 2 * way
                 held_at = 0 if distance < 3 else distance - 1
@@ -474,36 +484,48 @@
 
                 @pl.when(inside(source) & inside(there))
                 def _(way=way, source=source):
-                    act(hop(way, distance, source))
-
-        each_hop(1, lambda copy: copy.start())
-        if rows > 2:
-            each_hop(2, lambda copy: copy.start())
-        image[...] = 0.5 * own[...].astype(jnp.float32)
-        extended[halo : halo + blocks] = own[...]
+                    act(hop(h, way, distance, source))
+
+        def begin(copy):
+            copy.start()
+
+        for h in range(HALVES):
+            for distance in range(1, min(rows, 3)):
+                each_hop(h, distance, begin)
+        image[...] = 0.5 * basis_or_first[a][...].astype(jnp.bfloat16).astype(jnp.float32)
+        for h in range(HALVES):
+            extended[halo : halo + blocks, parts_of[h]] = own[h]
         for copy in halos:
             copy.wait()
-        extended[0:halo] = left[...]
-        extended[halo + blocks :] = right[...]
+        for h in range(HALVES):
+            extended[0:halo, parts_of[h]] = left[h]
+            extended[halo + blocks :, parts_of[h]] = right[h]
         for g in range(near_groups):
             near_picked[g] = jnp.dot(
                 near_pick[g], extended[...], preferred_element_type=jnp.float32
             )
+        relays = [(h, distance) for distance in range(3, rows) for h in range(HALVES)]
+
+        def relay(h, distance):
+            arrive(h, distance - 1)
+            each_hop(h, distance, begin)
+
+        early = min(len(relays), near_groups - 1)
 
         @pl.loop(0, near_groups)
         def _(g):
             if a == 0:
                 load(0, g).wait()
             near_group(sides, g, near_picked, near_place, near_ref, near_out, image, 3 - a)
-
-        for distance in range(3, rows):
-            arrive(distance - 1)
-            each_hop(distance, lambda copy: copy.start())
-        for distance in sorted({1, rows - 1}):
-            arrive(distance)
-        for distance in range(1, rows):
-            each_hop(distance, lambda copy: copy.wait_send())
-        between()
+            for n in range(early):
+
+                @pl.when(g == near_groups - early + n)
+                def _(n=n):
+                    relay(*relays[n])
+
+        for step in relays[early:]:
+            relay(*step)
+        prepare()
         if a == 0:
             for kind in (1, 2):
 
@@ -511,18 +533,10 @@
                 def _(g, kind=kind):
                     load(kind, g).wait()
 
-        for g in range(groups):
-            far_picked[g] = jnp.dot(
-                far_pick[g],
-                everything[...].reshape(rows * blocks, width),
-                preferred_element_type=jnp.float32,
-            ).astype(jnp.bfloat16)
-
         far = functools.partial(
             far_group,
-            sides,
+            some,
             3 - a,
-            far_picked=far_picked,
             far_place=far_place,
             far_ranks=far_ranks,
             far_left=far_left,
@@ -530,32 +544,32 @@
             far_out=far_out,
         )
 
-        def pair_copy(k, q):
+        def pair_copy(h, k, q):
             return remote(
-                to_partner.at[q],
-                from_partner.at[q],
-                pair_send.at[a],
-                pair_recv.at[a],
+                to_partner.at[h, q],
+                from_partner.at[h, q],
+                pair_send.at[a, h],
+                pair_recv.at[a, h],
                 k,
                 (row, partner),
             )
 
-        def chip_copies(k, q, here):
+        def chip_copies(h, k, q, here):
             device = (row, 2 * q + core)
             return [
                 remote(
-                    code_to[a].at[q],
-                    code_from[a].at[here],
-                    chip_send.at[a],
-                    chip_recv.at[a],
+                    code_to[a].at[h, q],
+                    code_from[a].at[h, here],
+                    chip_send.at[a, h],
+                    chip_recv.at[a, h],
                     k,
                     device,
                 ),
                 remote(
-                    scale_to.at[a, q],
-                    scale_from.at[a, here],
-                    scale_send.at[a],
-                    scale_recv.at[a],
+                    scale_to.at[a, h, q],
+                    scale_from.at[a, h, here],
+                    scale_send.at[a, h],
+                    scale_recv.at[a, h],
                     k,
                     device,
                 ),
@@ -563,69 +577,90 @@
 
         top_code = WIDE if a == 0 else TOP
 
-        def pack(source, q):
+        def pack(h, q):
             lows = []
-            for s in range(sides):
-                value = source[q, :, lanes[s]]
+            for s in range(some):
+                value = to_chips[h, q, :, lanes[s]]
                 scale = jnp.maximum(jnp.max(jnp.abs(value), axis=0, keepdims=True), 1e-30)
-                scale_to[a, q, s * TILE : (s + 1) * TILE] = jnp.broadcast_to(scale, (TILE, LANES))
+                scale_to[a, h, q, s * TILE : (s + 1) * TILE] = jnp.broadcast_to(
+                    scale, (TILE, LANES)
+                )
                 code = to_code(value, scale, top_code)
                 if a == 0:
                     high = jnp.floor(code * (1.0 / BYTE))
                     lows.append(code - high * BYTE)
                     code = high
-                code_to[a][q, :, lanes[s]] = narrow(code)
+                code_to[a][h, q, :, lanes[s]] = narrow(code)
             for n in range(len(lows) // 2):
                 code = lows[2 * n] * BYTE + (lows[2 * n + 1] - BYTE * BYTE / 2)
-                code_to[a][q, :, width + n * LANES : width + (n + 1) * LANES] = narrow(code)
-
-        def unpack(q):
-            codes = [decode(code_from[a][q, :, lanes[s]]) for s in range(sides)]
+                code_to[a][h, q, :, lanes[some + n]] = narrow(code)
+
+        def unpack(h, q):
+            codes = [decode(code_from[a][h, q, :, lanes[s]]) for s in range(some)]
             if a == 0:
-                for n in range(sides // 2):
-                    both = decode(code_from[a][q, :, width + n * LANES : width + (n + 1) * LANES])
+                for n in range(some // 2):
+                    both = decode(code_from[a][h, q, :, lanes[some + n]])
                     both = both + BYTE * BYTE / 2
                     high = jnp.floor(both * (1.0 / BYTE))
                     codes[2 * n] = codes[2 * n] * BYTE + high
                     codes[2 * n + 1] = codes[2 * n + 1] * BYTE + (both - high * BYTE)
-            for s in range(sides):
-                scale = scale_from[a, q, s * TILE : s * TILE + 1] * (1.0 / top_code)
-                image[:, lanes[s]] += codes[s] * scale
-
-        @pl.loop(1, pairs + 2)
-        def _(t):
-            @pl.when(t <= pairs)
-            def _():
-                q = lax.rem(chip + t, pairs)
-                to_partner[q] = far(2 * q + 1 - core)
-                pair_copy(t - 1, q).start()
-
-            @pl.when(t > 1)
-            def _():
-                i = t - 1
+            for s in range(some):
+                scale = scale_from[a, h, q, s * TILE : s * TILE + 1] * (1.0 / top_code)
+                image[:, lanes[h * some + s]] += codes[s] * scale
+
+        for h in range(HALVES):
+            for distance in sorted({1, rows - 1}):
+                arrive(h, distance)
+            for g in range(groups):
+                far_picked[h, g] = jnp.dot(
+                    far_pick[g],
+                    everything[h].reshape(rows * blocks, part_width),
+                    preferred_element_type=jnp.float32,
+                ).astype(jnp.bfloat16)
+
+            @pl.loop(1, pairs + 2)
+            def _(t, h=h):
+                @pl.when(t <= pairs)
+                def _():
+                    q = lax.rem(chip + t, pairs)
+                    to_partner[h, q], to_chips[h, q] = far(
+                        [2 * q + 1 - core, 2 * q + core], far_picked=far_picked.at[h]
+                    )
+                    pair_copy(h, t - 1, q).start()
+
+                @pl.when(t > 1)
+                def _():
+                    i = t - 1
+                    q = lax.rem(chip + i, pairs)
+                    pair_copy(h, i - 1, q).wait_recv()
+                    to_chips[h, q] = to_chips[h, q] + from_partner[h, q]
+
+                    @pl.when(i < pairs)
+                    def _():
+                        pack(h, q)
+                        for copy in chip_copies(h, i - 1, q, chip):
+                            copy.start()
+
+            if h == HALVES - 1:
+                between()
+        for h in range(HALVES):
+            image[:, parts_of[h]] += to_chips[h, chip]
+            for i in range(1, pairs):
+                source = lax.rem(chip + pairs - i, pairs)
+                for copy in chip_copies(h, i - 1, source, source):
+                    copy.wait_recv()
+                unpack(h, source)
+        for h in range(HALVES):
+            for distance in range(1, rows):
+                each_hop(h, distance, lambda copy: copy.wait_send())
+            for i in range(1, pairs + 1):
                 q = lax.rem(chip + i, pairs)
-                to_chips[q] = far(2 * q + core)
-                pair_copy(i - 1, q).wait_recv()
-                to_chips[q] = to_chips[q] + from_partner[q]
-
-                @pl.when(i < pairs)
-                def _():
-                    pack(to_chips, q)
-                    for copy in chip_copies(i - 1, q, chip):
-                        copy.start()
-
-        image[...] += to_chips[chip]
-        for i in range(1, pairs):
-            source = lax.rem(chip + pairs - i, pairs)
-            for copy in chip_copies(i - 1, source, source):
-                copy.wait_recv()
-            unpack(source)
-        for i in range(1, pairs + 1):
-            q = lax.rem(chip + i, pairs)
-            pair_copy(i - 1, q).wait_send()
-            if i < pairs:
-                for copy in chip_copies(i - 1, q, chip):
-                    copy.wait_send()
+                pair_copy(h, i - 1, q).wait_send()
+                if i < pairs:
+                    for copy in chip_copies(h, i - 1, q, chip):
+                        copy.wait_send()
+
+    basis_or_first = (first_ref, basis)
 
     def slot_codes(value, scales, buffer):
         for s in range(0, sides, 2):
@@ -659,7 +694,7 @@
                 )
         return values
 
-    operate(0, lambda: None)
+    operate(0, lambda: None, lambda: None)
     found = [[] for _ in range(7)]
     for s in range(sides):
         one, two = first_ref[:, lanes[s]], image[:, lanes[s]]
@@ -693,7 +728,7 @@
         )
         value = (image[:, lanes[s]] - project * first_ref[:, lanes[s]]) / norm
         basis[:, lanes[s]] = value
-        own[:, lanes[s]] = value.astype(jnp.bfloat16)
+        own[s // some, :, lanes[s % some]] = value.astype(jnp.bfloat16)
         bound = (top_image + jnp.abs(project) * top_first) / norm
         basis_scale = basis_scale + jnp.where(iota((count, LANES), 1) == s, bound, 0.0)
         projects.append(project)
@@ -705,11 +740,10 @@
     basis_start, basis_recv, basis_send = to_all(1, sent_basis, landed_basis, every)
     image_start, image_recv, image_send = to_all(2, sent_image, landed_image, every)
 
-    def send_basis():
+    def code_basis():
         slot_codes(basis[...], [single(mine_scale, s) for s in range(sides)], sent_basis)
-        basis_start()
-
-    operate(1, send_basis)
+
+    operate(1, code_basis, basis_start)
     scales = [largest(image[:, lanes[s]]) for s in range(sides)]
     slot_codes(image[...], scales, sent_image)
     image_start()
@@ -771,6 +805,7 @@
     near_count, far_count = near_blocks.shape[1], far_left.shape[1]
     halo = blocks // 4
     pairs = columns // 2
+    part = width // HALVES
     dma = pltpu.SemaphoreType.DMA
     real, half, code = jnp.float32, jnp.bfloat16, jnp.int16
     out_slots = (count, sides * capacity + TILE, lanes)
@@ -792,7 +827,7 @@
             pltpu.VMEM((columns, far_count, rows * blocks), half),
             pltpu.VMEM((columns, blocks, far_count), half),
             pltpu.VMEM((columns, far_count, lanes), real),
-            pltpu.VMEM((columns, far_count, width), half),
+            pltpu.VMEM((HALVES, columns, far_count, part), half),
             pltpu.VMEM(out_slots, real),
             pltpu.VMEM(out_slots, real),
             pltpu.VMEM(code_slots, code),
@@ -803,37 +838,37 @@
             pltpu.VMEM(near_blocks.shape, half),
             pltpu.VMEM(far_left.shape, half),
             pltpu.VMEM(far_right.shape, half),
-            pltpu.VMEM((blocks, width), half),
+            pltpu.VMEM((HALVES, blocks, part), half),
             pltpu.VMEM((blocks, width), real),
             pltpu.VMEM((blocks, width), real),
-            pltpu.VMEM((rows, blocks, width), half),
+            pltpu.VMEM((HALVES, rows, blocks, part), half),
             pltpu.VMEM((blocks + 2 * halo, width), half),
-            pltpu.VMEM((halo, width), half),
-            pltpu.VMEM((halo, width), half),
-            pltpu.VMEM((near_blocks.shape[1], width), real),
-            pltpu.VMEM((far_left.shape[1], width), real),
-            pltpu.VMEM((pairs, blocks, width), real),
-            pltpu.VMEM((pairs, blocks, width), real),
-            pltpu.VMEM((pairs, blocks, width), real),
-            pltpu.VMEM((pairs, blocks, 3 * width // 2), code),
-            pltpu.VMEM((pairs, blocks, 3 * width // 2), code),
-            pltpu.VMEM((pairs, blocks, width), code),
-            pltpu.VMEM((pairs, blocks, width), code),
-            pltpu.VMEM((2, pairs, sides * TILE, lanes), real),
-            pltpu.VMEM((2, pairs, sides * TILE, lanes), real),
+            pltpu.VMEM((HALVES, halo, part), half),
+            pltpu.VMEM((HALVES, halo, part), half),
+            pltpu.VMEM((near_count, width), real),
+            pltpu.VMEM((2, far_count, part), real),
+            pltpu.VMEM((HALVES, pairs, blocks, part), real),
+            pltpu.VMEM((HALVES, pairs, blocks, part), real),
+            pltpu.VMEM((HALVES, pairs, blocks, part), real),
+            pltpu.VMEM((HALVES, pairs, blocks, 3 * part // 2), code),
+            pltpu.VMEM((HALVES, pairs, blocks, 3 * part // 2), code),
+            pltpu.VMEM((HALVES, pairs, blocks, part), code),
+            pltpu.VMEM((HALVES, pairs, blocks, part), code),
+            pltpu.VMEM((2, HALVES, pairs, sides // HALVES * TILE, lanes), real),
+            pltpu.VMEM((2, HALVES, pairs, sides // HALVES * TILE, lanes), real),
             pltpu.VMEM((2, TILE, lanes), real),
             pltpu.VMEM((2, count, TILE, lanes), real),
             dma((3, max(columns, near_groups))),
             dma((2, 2)),
             dma((2, 2)),
-            dma((2, 2, rows - 1)),
-            dma((2, 2, rows - 1)),
-            dma((2, pairs)),
-            dma((2, pairs)),
-            dma((2, pairs)),
-            dma((2, pairs)),
-            dma((2, pairs)),
-            dma((2, pairs)),
+            dma((2, HALVES, 2, rows - 1)),
+            dma((2, HALVES, 2, rows - 1)),
+            dma((2, HALVES, pairs)),
+            dma((2, HALVES, pairs)),
+            dma((2, HALVES, pairs)),
+            dma((2, HALVES, pairs)),
+            dma((2, HALVES, pairs)),
+            dma((2, HALVES, pairs)),
             dma((5,)),
             dma((5,)),
         ],

time: 102 us -> 98.9 us (0.970)
  Pallas kernels: 96.2 us -> 93.3 us
    pallas_call x1, Pallas kernels: 96.2 us -> 93.3 us  [body(): pl.pallas_call(functools.partial(arnoldi_kernel, rows, columns), out_shap...]
where the time goes in v4:
time: 98.9 us; the launch traced here: 98.7 us
  Pallas kernels  93.3 us (94%)
  other arithmetic  3.52 us (4%)
  local copies, waits for them, and re-layouts  1.26 us (1%)
    pallas_call x1, Pallas kernels, body(): pl.pallas_call(functools.partial(arnoldi_kernel, rows, columns), out_shap...  93.3 us

profile of v4, /device:TPU:0, one launch (start us, length us, event | category | flops | bytes accessed | tf_op | source)
XLA Modules:
  0.0 98.7 jit_solution(1124046791327022141)
XLA Ops:
  0.6 93.3 %shard_map.121 = (f32[512,128]{1,0:T(8,128)}, f32[512,128]{1,0:T(8,128)}, f32[512,128]{1,0:T(8,128)}, f32[512,128]{1,0:T(8,128)}, f32[4,5]{1,0:T(4,128)}) custom-call(f32[512,128]{1,0:T(8,128)} %bitcast.16, s32[1,128]{1,0:T(1,128)} %bitcast.25, s32[3,128]{1,0:T(4,128)} %bitcast.23, s32[3,128]{1,0:T(4,128)} %bitcast.24, s32[8,128]{1,0:T(8,128)} %bitcast.19, ...), custom_call_target="tpu_custom_call" | custom-call | tf_op jit(solution)/shard_map/pallas_call | solution.py:814
  93.9 1.8 %add.3 = f32[512,128]{1,0:T(8,128)} add(f32[512,128]{1,0:T(8,128)} %get-tuple-element.8, f32[512,128]{1,0:T(8,128)} %get-tuple-element.9) | non-fusion elementwise | flops 65536 | bytes 786432 | tf_op jit(solution)/shard_map/add | solution.py:892
  95.7 1.8 %sub.3 = f32[512,128]{1,0:T(8,128)} subtract(f32[512,128]{1,0:T(8,128)} %get-tuple-element.10, f32[512,128]{1,0:T(8,128)} %get-tuple-element.11) | non-fusion elementwise | flops 65536 | bytes 786432 | tf_op jit(solution)/shard_map/sub | solution.py:893
  97.4 1.3 %copy.14 = f32[5,4]{0,1:T(4,128)} copy(f32[5,4]{0,1:T(4,128)} %bitcast.22) | data formatting | bytes 160

commit v5 on v4

--- a/solution.py
+++ b/solution.py
@@ -490,11 +490,15 @@
             copy.start()
 
         for h in range(HALVES):
-            for distance in range(1, min(rows, 3)):
+            for distance in reversed(range(1, min(rows, 3))):
                 each_hop(h, distance, begin)
         image[...] = 0.5 * basis_or_first[a][...].astype(jnp.bfloat16).astype(jnp.float32)
         for h in range(HALVES):
             extended[halo : halo + blocks, parts_of[h]] = own[h]
+        for distance in range(3, rows):
+            for h in range(HALVES):
+                arrive(h, distance - 1)
+                each_hop(h, distance, begin)
         for copy in halos:
             copy.wait()
         for h in range(HALVES):
@@ -504,27 +508,12 @@
             near_picked[g] = jnp.dot(
                 near_pick[g], extended[...], preferred_element_type=jnp.float32
             )
-        relays = [(h, distance) for distance in range(3, rows) for h in range(HALVES)]
-
-        def relay(h, distance):
-            arrive(h, distance - 1)
-            each_hop(h, distance, begin)
-
-        early = min(len(relays), near_groups - 1)
-
-        @pl.loop(0, near_groups)
-        def _(g):
+
+        def near(g):
             if a == 0:
                 load(0, g).wait()
             near_group(sides, g, near_picked, near_place, near_ref, near_out, image, 3 - a)
-            for n in range(early):
-
-                @pl.when(g == near_groups - early + n)
-                def _(n=n):
-                    relay(*relays[n])
-
-        for step in relays[early:]:
-            relay(*step)
+
         prepare()
         if a == 0:
             for kind in (1, 2):
@@ -618,19 +607,19 @@
                     preferred_element_type=jnp.float32,
                 ).astype(jnp.bfloat16)
 
-            @pl.loop(1, pairs + 2)
-            def _(t, h=h):
-                @pl.when(t <= pairs)
-                def _():
-                    q = lax.rem(chip + t, pairs)
-                    to_partner[h, q], to_chips[h, q] = far(
-                        [2 * q + 1 - core, 2 * q + core], far_picked=far_picked.at[h]
-                    )
-                    pair_copy(h, t - 1, q).start()
-
-                @pl.when(t > 1)
-                def _():
-                    i = t - 1
+            for t in range(1, pairs + 1, 2):
+                chosen = [lax.rem(chip + n, pairs) for n in (t, t + 1)]
+                found = far(
+                    [2 * q + 1 - core for q in chosen] + [2 * q + core for q in chosen],
+                    far_picked=far_picked.at[h],
+                )
+                for n, q in enumerate(chosen):
+                    to_partner[h, q] = found[n]
+                    pair_copy(h, t + n - 1, q).start()
+                    to_chips[h, q] = found[2 + n]
+
+                @pl.loop(t - 2 if t > 1 else 1, t if t < pairs - 1 else pairs + 1)
+                def _(i, h=h):
                     q = lax.rem(chip + i, pairs)
                     pair_copy(h, i - 1, q).wait_recv()
                     to_chips[h, q] = to_chips[h, q] + from_partner[h, q]
@@ -643,6 +632,11 @@
 
             if h == HALVES - 1:
                 between()
+
+                @pl.loop(0, near_groups)
+                def _(g):
+                    near(g)
+
         for h in range(HALVES):
             image[:, parts_of[h]] += to_chips[h, chip]
             for i in range(1, pairs):
@@ -846,7 +840,7 @@
             pltpu.VMEM((HALVES, halo, part), half),
             pltpu.VMEM((HALVES, halo, part), half),
             pltpu.VMEM((near_count, width), real),
-            pltpu.VMEM((2, far_count, part), real),
+            pltpu.VMEM((4, far_count, part), real),
             pltpu.VMEM((HALVES, pairs, blocks, part), real),
             pltpu.VMEM((HALVES, pairs, blocks, part), real),
             pltpu.VMEM((HALVES, pairs, blocks, part), real),

time: 98.9 us -> 94.5 us (0.956)
  Pallas kernels: 93.3 us -> 88.9 us
    pallas_call x1, Pallas kernels: 93.3 us -> 88.9 us  [body(): pl.pallas_call(functools.partial(arnoldi_kernel, rows, columns), out_shap...]
where the time goes in v5:
time: 94.5 us; the launch traced here: 94.3 us
  Pallas kernels  88.9 us (94%)
  other arithmetic  3.52 us (4%)
  local copies, waits for them, and re-layouts  1.26 us (1%)
    pallas_call x1, Pallas kernels, body(): pl.pallas_call(functools.partial(arnoldi_kernel, rows, columns), out_shap...  88.9 us

profile of v5, /device:TPU:0, one launch (start us, length us, event | category | flops | bytes accessed | tf_op | source)
XLA Modules:
  0.0 94.3 jit_solution(14094601615296374799)
XLA Ops:
  0.6 88.9 %shard_map.121 = (f32[512,128]{1,0:T(8,128)}, f32[512,128]{1,0:T(8,128)}, f32[512,128]{1,0:T(8,128)}, f32[512,128]{1,0:T(8,128)}, f32[4,5]{1,0:T(4,128)}) custom-call(f32[512,128]{1,0:T(8,128)} %bitcast.16, s32[1,128]{1,0:T(1,128)} %bitcast.25, s32[3,128]{1,0:T(4,128)} %bitcast.23, s32[3,128]{1,0:T(4,128)} %bitcast.24, s32[8,128]{1,0:T(8,128)} %bitcast.19, ...), custom_call_target="tpu_custom_call" | custom-call | tf_op jit(solution)/shard_map/pallas_call | solution.py:808
  89.6 1.8 %add.3 = f32[512,128]{1,0:T(8,128)} add(f32[512,128]{1,0:T(8,128)} %get-tuple-element.8, f32[512,128]{1,0:T(8,128)} %get-tuple-element.9) | non-fusion elementwise | flops 65536 | bytes 786432 | tf_op jit(solution)/shard_map/add | solution.py:886
  91.3 1.8 %sub.3 = f32[512,128]{1,0:T(8,128)} subtract(f32[512,128]{1,0:T(8,128)} %get-tuple-element.10, f32[512,128]{1,0:T(8,128)} %get-tuple-element.11) | non-fusion elementwise | flops 65536 | bytes 786432 | tf_op jit(solution)/shard_map/sub | solution.py:887
  93.1 1.3 %copy.14 = f32[5,4]{0,1:T(4,128)} copy(f32[5,4]{0,1:T(4,128)} %bitcast.22) | data formatting | bytes 160

commit v6 on v5

--- a/solution.py
+++ b/solution.py
@@ -630,8 +630,9 @@
                         for copy in chip_copies(h, i - 1, q, chip):
                             copy.start()
 
+            if h == 0:
+                between()
             if h == HALVES - 1:
-                between()
 
                 @pl.loop(0, near_groups)
                 def _(g):

time: 94.5 us -> 94.4 us (level)
  no operation moved by 1% of the time
where the time goes in v6:
time: 94.4 us; the launch traced here: 94.2 us
  Pallas kernels  88.8 us (94%)
  other arithmetic  3.52 us (4%)
  local copies, waits for them, and re-layouts  1.26 us (1%)
    pallas_call x1, Pallas kernels, body(): pl.pallas_call(functools.partial(arnoldi_kernel, rows, columns), out_shap...  88.8 us

profile of v6, /device:TPU:0, one launch (start us, length us, event | category | flops | bytes accessed | tf_op | source)
XLA Modules:
  0.0 94.2 jit_solution(14025425973874590647)
XLA Ops:
  0.6 88.8 %shard_map.121 = (f32[512,128]{1,0:T(8,128)}, f32[512,128]{1,0:T(8,128)}, f32[512,128]{1,0:T(8,128)}, f32[512,128]{1,0:T(8,128)}, f32[4,5]{1,0:T(4,128)}) custom-call(f32[512,128]{1,0:T(8,128)} %bitcast.16, s32[1,128]{1,0:T(1,128)} %bitcast.25, s32[3,128]{1,0:T(4,128)} %bitcast.23, s32[3,128]{1,0:T(4,128)} %bitcast.24, s32[8,128]{1,0:T(8,128)} %bitcast.19, ...), custom_call_target="tpu_custom_call" | custom-call | tf_op jit(solution)/shard_map/pallas_call | solution.py:809
  89.4 1.8 %add.3 = f32[512,128]{1,0:T(8,128)} add(f32[512,128]{1,0:T(8,128)} %get-tuple-element.8, f32[512,128]{1,0:T(8,128)} %get-tuple-element.9) | non-fusion elementwise | flops 65536 | bytes 786432 | tf_op jit(solution)/shard_map/add | solution.py:887
  91.2 1.8 %sub.3 = f32[512,128]{1,0:T(8,128)} subtract(f32[512,128]{1,0:T(8,128)} %get-tuple-element.10, f32[512,128]{1,0:T(8,128)} %get-tuple-element.11) | non-fusion elementwise | flops 65536 | bytes 786432 | tf_op jit(solution)/shard_map/sub | solution.py:888
  93.0 1.3 %copy.14 = f32[5,4]{0,1:T(4,128)} copy(f32[5,4]{0,1:T(4,128)} %bitcast.22) | data formatting | bytes 160
